TPU v7x, 32 devices: a whole 2x2x4 slice. The times are simulated.
32 devices in a mesh: mp: 2 (over core), heads: 8 (over z, y), tok: 2 (over x).
Axes of the slice: x: 2, y: 2, z: 4, core: 2. Of those that a mesh axis runs over, the one named last changes fastest.
Arguments:
- context: bfloat16 [2, 512, 8192], P('mp', None, 'heads'), may hold values from -6 to 6
- out_weight: bfloat16 [2, 8192, 8192], P('mp', 'heads', 'tok'), may hold values from -0.0625 to 0.0625
- skip_states: bfloat16 [2, 512, 8192], P(None, None, 'tok'), may hold values from -6 to 6
- gram_old: float32 [8192, 8192], P('tok', ('mp', 'heads')), may hold values from -1 to 3
- cross_old: float32 [8192, 8192], P('tok', ('mp', 'heads')), may hold values from -30 to 30
- map_old: float32 [8192, 8192], P('tok', ('mp', 'heads')), may hold values from -0.3 to 0.3
Outputs:
- gram_new: float32 [8192, 8192], P('tok', ('mp', 'heads'))
- cross_new: float32 [8192, 8192], P('tok', ('mp', 'heads'))
- map_new: float32 [8192, 8192], P('tok', ('mp', 'heads'))
- residual_new: float32 [8192, 8192], P('tok', ('mp', 'heads'))
All inputs are finite; a program needn't handle non-finite values.
Results may differ from a plain program's by a relative error of at most 0.03.
Values may be sent and summed in bfloat16 or wider, within the bound.
A program may use at most 256 MiB of HBM per device.

v0:
```python
import jax
import jax.numpy as jnp
from jax import lax
from jax.sharding import PartitionSpec as P

decay_keep = 0.75
ridge_weight = 0.1
f32, bf16 = jnp.float32, jnp.bfloat16
CHUNKS = 4


def dot(a, b):
    return jnp.dot(a, b, preferred_element_type=f32)


def token_inner(left, right):
    return lax.dot_general(left, right, (((0,), (0,)), ((), ())), preferred_element_type=f32)


def shifted(block, axis, shift):
    n = lax.axis_size(axis)
    return lax.ppermute(block, axis, [(i, (i + shift) % n) for i in range(n)])


def total_over(value, axis):
    n = lax.axis_size(axis)
    if n & (n - 1):
        return lax.psum(value, axis)
    bit = 1
    while bit < n:
        value = value + lax.ppermute(value, axis, [(i, i ^ bit) for i in range(n)])
        bit *= 2
    return value


def sum_tok(value):
    n = lax.axis_size("tok")
    half = value.astype(bf16)
    for shift in range(1, n):
        value = value + shifted(half, "tok", shift).astype(f32)
    return value.astype(bf16)


def scatter_sum(part, axis):
    n = lax.axis_size(axis)
    me = lax.axis_index(axis)
    share = part.shape[1] // n
    blocks = [part[:, i * share:(i + 1) * share] for i in range(n)]
    bit = 1
    while bit < n:
        mine = (me // bit) % 2 == 1
        keep = [jnp.where(mine, high, low) for low, high in zip(blocks[0::2], blocks[1::2])]
        send = [jnp.where(mine, low, high) for low, high in zip(blocks[0::2], blocks[1::2])]
        send = jnp.concatenate([block.astype(bf16) for block in send], 1)
        got = lax.ppermute(send, axis, [(i, i ^ bit) for i in range(n)]).astype(f32)
        blocks = [block.astype(f32) + got[:, i * share:(i + 1) * share] for i, block in enumerate(keep)]
        bit *= 2
    return blocks[0]


def gather_columns(block, axis):
    n = lax.axis_size(axis)
    me = lax.axis_index(axis)
    bit = n // 2
    blocks = [block]
    while bit:
        mine = (me // bit) % 2 == 1
        own = jnp.concatenate(blocks, 1)
        got = lax.ppermute(own, axis, [(i, i ^ bit) for i in range(n)])
        share = block.shape[1]
        got = [got[:, i * share:(i + 1) * share] for i in range(len(blocks))]
        low = [jnp.where(mine, g, o) for g, o in zip(got, blocks)]
        high = [jnp.where(mine, o, g) for g, o in zip(got, blocks)]
        blocks = [x for pair in zip(low, high) for x in pair]
        bit //= 2
    return jnp.concatenate(blocks, 1)


def make_states(context, out_weight, skip_states, width):
    n_tok, n_heads, n_mp = (lax.axis_size(a) for a in ("tok", "heads", "mp"))
    t, h, k = (lax.axis_index(a) for a in ("tok", "heads", "mp"))
    tokens, features = skip_states.shape[1:]
    share = features // n_heads
    part = dot(context[0], out_weight[0]).astype(bf16)
    mine = scatter_sum(part, "heads")
    skip = lax.dynamic_slice(skip_states, (k, 0, h * share), (1, tokens, share))[0]
    mine = (mine + skip.astype(f32)).astype(bf16)
    other = lax.ppermute(mine, "mp", [(0, 1), (1, 0)])
    pair = jnp.stack([jnp.where(k == 0, mine, other), jnp.where(k == 0, other, mine)])
    if share == width and n_tok == n_mp == 2:
        away = lax.ppermute(pair, ("mp", "tok"), [(0, 1), (3, 2)])
        columns = jnp.where(k == t, pair, away)
        half = lax.dynamic_slice_in_dim(pair[0], k * (tokens // 2), tokens // 2, 0)
        rows = gather_columns(half, "heads")
        rows_other = lax.ppermute(rows, "mp", [(0, 1), (1, 0)])
        first = jnp.where(k == 0, rows, rows_other)
        second = jnp.where(k == 0, rows_other, rows)
        source = jnp.concatenate([first, second], 0)
        return source, columns[0], columns[1]
    both = lax.all_gather(pair, "heads", axis=2, tiled=True)
    whole = lax.all_gather(both, "tok", axis=2, tiled=True)
    columns = lax.dynamic_slice_in_dim(whole, (k * n_heads + h) * width, width, 2)
    return both[0], columns[0], columns[1]


def per_device(context, out_weight, skip_states, gram_old, cross_old, map_old):
    n_tok = lax.axis_size("tok")
    t = lax.axis_index("tok")
    tokens = context.shape[1]
    height, width = gram_old.shape
    new_weight = (1.0 - decay_keep) / tokens
    step = height // CHUNKS
    cuts = [slice(c * step, (c + 1) * step) for c in range(CHUNKS)]

    map_half = map_old.astype(bf16)
    gram_old_half = gram_old.astype(bf16)
    gram_old_half, context = lax.optimization_barrier((gram_old_half, context))
    panel = lax.all_gather(gram_old_half, ("mp", "heads"), axis=1, tiled=True)
    maps = [map_half] + [shifted(map_half, "tok", s) for s in range(1, n_tok)]
    source, source_cols, target_cols = make_states(context, out_weight, skip_states, width)

    gram_new = decay_keep * gram_old + new_weight * token_inner(source, source_cols)
    cross_new = decay_keep * cross_old + new_weight * token_inner(source, target_cols)

    def panel_part(cut, s):
        owner = lax.rem(t - s + n_tok, n_tok)
        return lax.dynamic_slice(panel, (cut.start, owner * height), (step, height))

    inner_map = sum_tok(dot(source, map_half))
    residuals, halves = [], []
    for cut in cuts:
        product = sum(dot(panel_part(cut, s), maps[s]) for s in range(n_tok))
        low_rank = token_inner(source[:, cut], inner_map)
        residual = (
            cross_new[cut] - decay_keep * product - new_weight * low_rank - ridge_weight * map_old[cut]
        )
        residuals.append(residual)
        halves.append(residual.astype(bf16))
    away = [[shifted(half, "tok", s) for half in halves] for s in range(1, n_tok)]
    inner_residual = sum_tok(sum(dot(source[:, cut], half) for cut, half in zip(cuts, halves)))
    blocks = [jnp.concatenate(halves, 0)] + [jnp.concatenate(a, 0) for a in away]
    applied, squares, mixed = [], 0.0, 0.0
    for cut, residual in zip(cuts, residuals):
        product = sum(dot(panel_part(cut, s), blocks[s]) for s in range(n_tok))
        low_rank = token_inner(source[:, cut], inner_residual)
        value = decay_keep * product + new_weight * low_rank + ridge_weight * residual
        applied.append(value)
        squares = squares + jnp.sum(residual * residual)
        mixed = mixed + jnp.sum(residual * value)
    totals = jnp.stack([squares, mixed])
    for axis in ("mp", "tok", "heads"):
        totals = total_over(totals, axis)
    step_size = totals[0] / totals[1]
    residual = jnp.concatenate(residuals, 0)
    return (
        gram_new,
        cross_new,
        map_old + step_size * residual,
        residual - step_size * jnp.concatenate(applied, 0),
    )


def solution(mesh):
    block = P("tok", ("mp", "heads"))
    placed = (P("mp", None, "heads"), P("mp", "heads", "tok"), P(None, None, "tok"), block, block, block)
    return jax.shard_map(
        per_device, mesh=mesh, in_specs=placed, out_specs=(block,) * 4, check_vma=False
    )
```

profile of v0, /device:TPU:0, one launch (start us, length us, event | category | flops | bytes accessed | tf_op | source)
XLA Modules:
  0.0 658.0 jit_solution(4569896277670211610)
XLA Ops:
  7.2 6.0 convert_element_type.78
  13.3 8.1 %fusion.35 = bf16[512,4096]{1,0:T(8,128)(2,1)S(1)} fusion(bf16[1,1024,4096]{2,1,0:T(8,128)(2,1)} %param.7, bf16[1,512,1024]{2,1,0:T(8,128)(2,1)S(1)} %copy-done), kind=kOutput, calls=%fused_computation.49 | convolution fusion | flops 4297064448 | bytes 13631488 | tf_op jit(solution)/shard_map/dot_general | solution.py:13
  28.1 91.4 %collective-permute-done = bf16[512,2048]{1,0:T(8,128)(2,1)S(1)} collective-permute-done((bf16[512,2048]{1,0:T(8,128)(2,1)}, bf16[512,2048]{1,0:T(8,128)(2,1)S(1)}, u32[]{:S(2)}, u32[]{:S(2)}) %collective-permute-start) | collective-permute-done | bytes 2097184 | tf_op jit(solution)/shard_map/ppermute | solution.py:55
  122.3 48.0 %collective-permute-done.1 = bf16[512,1024]{1,0:T(8,128)(2,1)S(1)} collective-permute-done((bf16[512,1024]{1,0:T(8,128)(2,1)S(1)}, bf16[512,1024]{1,0:T(8,128)(2,1)S(1)}, u32[]{:S(2)}, u32[]{:S(2)}) %collective-permute-start.1) | collective-permute-done | bytes 1048608 | tf_op jit(solution)/shard_map/ppermute | solution.py:55
  170.6 5.1 select_convert_fusion
  177.6 35.3 %collective-permute-done.2 = bf16[512,512]{1,0:T(8,128)(2,1)S(1)} collective-permute-done((bf16[512,512]{1,0:T(8,128)(2,1)S(1)}, bf16[512,512]{1,0:T(8,128)(2,1)S(1)}, u32[]{:S(2)}, u32[]{:S(2)}) %collective-permute-start.2) | collective-permute-done | bytes 524320 | tf_op jit(solution)/shard_map/ppermute | solution.py:55
  216.4 20.9 %collective-permute-done.4 = bf16[256,512]{1,0:T(8,128)(2,1)S(1)} collective-permute-done((bf16[256,512]{1,0:T(8,128)(2,1)S(1)}, bf16[256,512]{1,0:T(8,128)(2,1)S(1)}, u32[]{:S(2)}, u32[]{:S(2)}) %collective-permute-start.4) | collective-permute-done | bytes 262176 | tf_op jit(solution)/shard_map/ppermute | solution.py:69
  237.6 25.5 %collective-permute-done.5 = bf16[256,1024]{1,0:T(8,128)(2,1)S(1)} collective-permute-done((bf16[256,1024]{1,0:T(8,128)(2,1)S(1)}, bf16[256,1024]{1,0:T(8,128)(2,1)S(1)}, u32[]{:S(2)}, u32[]{:S(2)}) %collective-permute-start.5) | collective-permute-done | bytes 524320 | tf_op jit(solution)/shard_map/ppermute | solution.py:69
  265.4 45.9 %collective-permute-done.6 = bf16[256,2048]{1,0:T(8,128)(2,1)S(1)} collective-permute-done((bf16[256,2048]{1,0:T(8,128)(2,1)S(1)}, bf16[256,2048]{1,0:T(8,128)(2,1)S(1)}, u32[]{:S(2)}, u32[]{:S(2)}) %collective-permute-start.6) | collective-permute-done | bytes 1048608 | tf_op jit(solution)/shard_map/ppermute | solution.py:69
  313.3 4.5 collective-permute-start.8
  320.4 17.1 %collective-permute-done.8 = bf16[2,512,512]{2,1,0:T(8,128)(2,1)} collective-permute-done((bf16[2,512,512]{2,1,0:T(8,128)(2,1)}, bf16[2,512,512]{2,1,0:T(8,128)(2,1)}, u32[]{:S(2)}, u32[]{:S(2)}) %collective-permute-start.8) | collective-permute-done | bytes 1048608 | tf_op jit(solution)/shard_map/ppermute | solution.py:91
  339.9 5.4 fusion.78
  349.5 5.3 multiply_add_fusion.2
  354.8 4.9 multiply_add_fusion.1
  361.4 69.0 %collective-permute-done.10 = bf16[512,512]{1,0:T(8,128)(2,1)S(1)} collective-permute-done((bf16[512,512]{1,0:T(8,128)(2,1)S(1)}, bf16[512,512]{1,0:T(8,128)(2,1)S(1)}, u32[]{:S(2)}, u32[]{:S(2)}) %collective-permute-start.10) | collective-permute-done | bytes 524320 | tf_op jit(solution)/shard_map/ppermute | solution.py:22
  430.7 8.3 %fusion.25 = f32[1024,512]{1,0:T(8,128)S(1)} fusion(bf16[4096,512]{1,0:T(8,128)(2,1)} %convert_element_type.93, bf16[4096,8192]{1,0:T(8,128)(2,1)} %all-gather.2.cloned.1.call-done, s32[]{:T(128)S(6)} %select_n.271), kind=kOutput, calls=%fused_computation.30 | convolution fusion | flops 4294967296 | bytes 14680068 | tf_op jit(solution)/shard_map/dot_general | solution.py:13
  439.0 8.3 %fusion.21 = f32[1024,512]{1,0:T(8,128)S(1)} fusion(bf16[4096,512]{1,0:T(8,128)(2,1)} %collective-permute-done.9, bf16[4096,8192]{1,0:T(8,128)(2,1)} %all-gather.2.cloned.1.call-done, s32[]{:T(128)S(6)} %select_n.272), kind=kOutput, calls=%fused_computation.26 | convolution fusion | flops 4294967296 | bytes 14680068 | tf_op jit(solution)/shard_map/dot_general | solution.py:13
  455.0 8.1 %fusion.13 = f32[1024,512]{1,0:T(8,128)S(1)} fusion(bf16[4096,512]{1,0:T(8,128)(2,1)} %collective-permute-done.9, bf16[4096,8192]{1,0:T(8,128)(2,1)} %all-gather.2.cloned.1.call-done, s32[]{:T(128)S(6)} %select_n.272), kind=kOutput, calls=%fused_computation.18 | convolution fusion | flops 4294967296 | bytes 14680068 | tf_op jit(solution)/shard_map/dot_general | solution.py:13
  463.2 8.2 %fusion.17 = f32[1024,512]{1,0:T(8,128)S(1)} fusion(bf16[4096,512]{1,0:T(8,128)(2,1)} %convert_element_type.93, bf16[4096,8192]{1,0:T(8,128)(2,1)} %all-gather.2.cloned.1.call-done, s32[]{:T(128)S(6)} %select_n.271), kind=kOutput, calls=%fused_computation.22 | convolution fusion | flops 4294967296 | bytes 14680068 | tf_op jit(solution)/shard_map/dot_general | solution.py:13
  478.0 8.3 %fusion.5 = f32[1024,512]{1,0:T(8,128)S(1)} fusion(bf16[4096,512]{1,0:T(8,128)(2,1)} %collective-permute-done.9, bf16[4096,8192]{1,0:T(8,128)(2,1)} %all-gather.2.cloned.1.call-done, s32[]{:T(128)S(6)} %select_n.272), kind=kOutput, calls=%fused_computation.10 | convolution fusion | flops 4294967296 | bytes 14680068 | tf_op jit(solution)/shard_map/dot_general | solution.py:13
  486.3 8.2 %fusion.9 = f32[1024,512]{1,0:T(8,128)S(1)} fusion(bf16[4096,512]{1,0:T(8,128)(2,1)} %convert_element_type.93, bf16[4096,8192]{1,0:T(8,128)(2,1)} %all-gather.2.cloned.1.call-done, s32[]{:T(128)S(6)} %select_n.271), kind=kOutput, calls=%fused_computation.14 | convolution fusion | flops 4294967296 | bytes 14680068 | tf_op jit(solution)/shard_map/dot_general | solution.py:13
  501.6 8.1 %fusion.29 = f32[1024,512]{1,0:T(8,128)S(1)} fusion(bf16[4096,512]{1,0:T(8,128)(2,1)} %collective-permute-done.9, bf16[4096,8192]{1,0:T(8,128)(2,1)} %all-gather.2.cloned.1.call-done, s32[]{:T(128)S(6)} %select_n.272), kind=kOutput, calls=%fused_computation.34 | convolution fusion | flops 4294967296 | bytes 14680068 | tf_op jit(solution)/shard_map/dot_general | solution.py:13
  509.8 10.6 %fusion.33 = f32[1024,512]{1,0:T(8,128)} fusion(bf16[4096,512]{1,0:T(8,128)(2,1)} %convert_element_type.93, bf16[4096,8192]{1,0:T(8,128)(2,1)} %all-gather.2.cloned.1.call-done, s32[]{:T(128)S(6)} %select_n.271), kind=kOutput, calls=%fused_computation.38 | convolution fusion | flops 4294967296 | bytes 14680068 | tf_op jit(solution)/shard_map/dot_general | solution.py:13
  526.3 8.8 %fusion.31 = f32[1024,512]{1,0:T(8,128)S(1)} fusion(bf16[4096,8192]{1,0:T(8,128)(2,1)} %all-gather.2.cloned.1.call-done, s32[]{:T(128)S(6)} %select_n.271, bf16[1024,512]{1,0:T(8,128)(2,1)} %get-tuple-element.46, bf16[1024,512]{1,0:T(8,128)(2,1)} %get-tuple-element.48, bf16[1024,512]{1,0:T(8,128)(2,1)} %get-tuple-element.50, ...), kind=kOutput, calls=%fused_computation.36 | convolution fusion | flops 4311744512 | bytes 14680068 | tf_op jit(solution)/shard_map/dot_general | solution.py:13
  535.1 9.1 %fusion.23 = f32[1024,512]{1,0:T(8,128)S(1)} fusion(bf16[4096,8192]{1,0:T(8,128)(2,1)} %all-gather.2.cloned.1.call-done, s32[]{:T(128)S(6)} %select_n.271, bf16[1024,512]{1,0:T(8,128)(2,1)} %get-tuple-element.46, bf16[1024,512]{1,0:T(8,128)(2,1)} %get-tuple-element.48, bf16[1024,512]{1,0:T(8,128)(2,1)} %get-tuple-element.50, ...), kind=kOutput, calls=%fused_computation.28 | convolution fusion | flops 4311744512 | bytes 14680068 | tf_op jit(solution)/shard_map/dot_general | solution.py:13
  544.2 10.0 %fusion.15 = f32[1024,512]{1,0:T(8,128)} fusion(bf16[4096,8192]{1,0:T(8,128)(2,1)} %all-gather.2.cloned.1.call-done, s32[]{:T(128)S(6)} %select_n.271, bf16[1024,512]{1,0:T(8,128)(2,1)} %get-tuple-element.46, bf16[1024,512]{1,0:T(8,128)(2,1)} %get-tuple-element.48, bf16[1024,512]{1,0:T(8,128)(2,1)} %get-tuple-element.50, ...), kind=kOutput, calls=%fused_computation.20 | convolution fusion | flops 4311744512 | bytes 14680068 | tf_op jit(solution)/shard_map/dot_general | solution.py:13
  554.2 10.0 %fusion.7 = f32[1024,512]{1,0:T(8,128)} fusion(bf16[4096,8192]{1,0:T(8,128)(2,1)} %all-gather.2.cloned.1.call-done, s32[]{:T(128)S(6)} %select_n.271, bf16[1024,512]{1,0:T(8,128)(2,1)} %get-tuple-element.46, bf16[1024,512]{1,0:T(8,128)(2,1)} %get-tuple-element.48, bf16[1024,512]{1,0:T(8,128)(2,1)} %get-tuple-element.50, ...), kind=kOutput, calls=%fused_computation.12 | convolution fusion | flops 4311744512 | bytes 14680068 | tf_op jit(solution)/shard_map/dot_general | solution.py:13
  568.4 8.4 %fusion.27 = f32[1024,512]{1,0:T(8,128)S(1)} fusion(bf16[4096,512]{1,0:T(8,128)(2,1)S(1)} %constant_dynamic-update-slice_fusion, bf16[4096,8192]{1,0:T(8,128)(2,1)} %all-gather.2.cloned.1.call-done, s32[]{:T(128)S(6)} %select_n.272), kind=kOutput, calls=%fused_computation.32 | convolution fusion | flops 4294967296 | bytes 14680068 | tf_op jit(solution)/shard_map/dot_general | solution.py:13
  580.0 7.2 %fusion.19 = f32[1024,512]{1,0:T(8,128)S(1)} fusion(bf16[4096,512]{1,0:T(8,128)(2,1)S(1)} %constant_dynamic-update-slice_fusion, bf16[4096,8192]{1,0:T(8,128)(2,1)} %all-gather.2.cloned.1.call-done, s32[]{:T(128)S(6)} %select_n.272), kind=kOutput, calls=%fused_computation.24 | convolution fusion | flops 4294967296 | bytes 14680068 | tf_op jit(solution)/shard_map/dot_general | solution.py:13
  591.7 8.3 %fusion.11 = f32[1024,512]{1,0:T(8,128)S(1)} fusion(bf16[4096,512]{1,0:T(8,128)(2,1)} %copy-done.24, bf16[4096,8192]{1,0:T(8,128)(2,1)} %all-gather.2.cloned.1.call-done, s32[]{:T(128)S(6)} %select_n.272), kind=kOutput, calls=%fused_computation.16 | convolution fusion | flops 4294967296 | bytes 14680068 | tf_op jit(solution)/shard_map/dot_general | solution.py:13
  603.8 8.3 %fusion.3 = f32[1024,512]{1,0:T(8,128)S(1)} fusion(bf16[4096,512]{1,0:T(8,128)(2,1)} %copy-done.24, bf16[4096,8192]{1,0:T(8,128)(2,1)} %all-gather.2.cloned.1.call-done, s32[]{:T(128)S(6)} %select_n.272), kind=kOutput, calls=%fused_computation.8 | convolution fusion | flops 4294967296 | bytes 14680068 | tf_op jit(solution)/shard_map/dot_general | solution.py:13
  636.7 14.1 %fusion = (f32[4096,512]{1,0:T(8,128)}, f32[4096,512]{1,0:T(8,128)}) fusion(f32[1024,512]{1,0:T(8,128)} %get-tuple-element.59, f32[1024,512]{1,0:T(8,128)} %get-tuple-element.58, f32[1024,512]{1,0:T(8,128)} %get-tuple-element.57, f32[1024,512]{1,0:T(8,128)} %get-tuple-element.56, f32[1024,512]{1,0:T(8,128)} %get-tuple-element.47, ...), kind=kLoop, calls=%fused_computation.2 | loop fusion | flops 20971520 | bytes 41943044 | tf_op jit(solution)/shard_map/sub | solution.py:159
  (162 shorter events, 91.6 us)
Async XLA Ops:
  7.2 423.5 %all-gather.2.cloned.1.call-start = ((), (), s32[]{:S(2)}) async-start(), calls=%async_computation | async-start | bytes 71303168 | tf_op jit(solution)/shard_map/all_gather | solution.py:118
  25.1 94.4 %collective-permute-start = (bf16[512,2048]{1,0:T(8,128)(2,1)}, bf16[512,2048]{1,0:T(8,128)(2,1)S(1)}, u32[]{:S(2)}, u32[]{:S(2)}) collective-permute-start(bf16[512,2048]{1,0:T(8,128)(2,1)} %pad_maximum_fusion.3), channel_id=1, source_target_pairs={{0,2},{2,0},{4,6},{6,4},{8,10},{10,8},{12,14},{14,12},{1,3},{3,1},... | collective-permute-start | bytes 6291464 | tf_op jit(solution)/shard_map/ppermute | solution.py:55
  28.1 92.0 %copy-start.5 = (bf16[512,4096]{1,0:T(8,128)(2,1)S(1)}, bf16[512,4096]{1,0:T(8,128)(2,1)}, u32[]{:S(2)}) copy-start(bf16[512,4096]{1,0:T(8,128)(2,1)} %copy-done.4) | copy-start | bytes 12582916
  122.2 48.1 %collective-permute-start.1 = (bf16[512,1024]{1,0:T(8,128)(2,1)S(1)}, bf16[512,1024]{1,0:T(8,128)(2,1)S(1)}, u32[]{:S(2)}, u32[]{:S(2)}) collective-permute-start(bf16[512,1024]{1,0:T(8,128)(2,1)S(1)} %pad_maximum_fusion.7), channel_id=1, source_target_pairs={{0,4},{2,6},{4,0},{6,2},{8,12},{10,14},{12,8},{14,10},{1,5},{3,7},... | collective-permute-start | bytes 3145736 | tf_op jit(solution)/shard_map/ppermute | solution.py:55
  175.7 37.2 %collective-permute-start.2 = (bf16[512,512]{1,0:T(8,128)(2,1)S(1)}, bf16[512,512]{1,0:T(8,128)(2,1)S(1)}, u32[]{:S(2)}, u32[]{:S(2)}) collective-permute-start(bf16[512,512]{1,0:T(8,128)(2,1)S(1)} %get-tuple-element.16), channel_id=1, source_target_pairs={{0,8},{2,10},{4,12},{6,14},{8,0},{10,2},{12,4},{14,6},{1,9},{3,11}... | collective-permute-start | bytes 1572872 | tf_op jit(solution)/shard_map/ppermute | solution.py:55
  214.3 2.0 collective-permute-start.3
  216.3 101.5 %slice-start = ((s8[8388608]{0:T(1024)(128)(4,1)}), s8[4194304]{0:T(1024)(128)(4,1)S(1)}, s32[]{:S(2)}) async-start(s8[8388608]{0:T(1024)(128)(4,1)} %bitcast.57), calls=%async_computation.1 | async-start | bytes 8388608
  216.4 20.9 %collective-permute-start.4 = (bf16[256,512]{1,0:T(8,128)(2,1)S(1)}, bf16[256,512]{1,0:T(8,128)(2,1)S(1)}, u32[]{:S(2)}, u32[]{:S(2)}) collective-permute-start(bf16[256,512]{1,0:T(8,128)(2,1)S(1)} %constant_dynamic-slice_fusion), channel_id=1, source_target_pairs={{0,8},{2,10},{4,12},{6,14},{8,0},{10,2},{12,4},{14,6},{1,9},{3,11}... | collective-permute-start | bytes 786440 | tf_op jit(solution)/shard_map/ppermute | solution.py:69
  237.5 25.6 %collective-permute-start.5 = (bf16[256,1024]{1,0:T(8,128)(2,1)S(1)}, bf16[256,1024]{1,0:T(8,128)(2,1)S(1)}, u32[]{:S(2)}, u32[]{:S(2)}) collective-permute-start(bf16[256,1024]{1,0:T(8,128)(2,1)S(1)} %pad_maximum_fusion.10), channel_id=1, source_target_pairs={{0,4},{2,6},{4,0},{6,2},{8,12},{10,14},{12,8},{14,10},{1,5},{3,7},... | collective-permute-start | bytes 1572872 | tf_op jit(solution)/shard_map/ppermute | solution.py:69
  263.3 54.5 %slice-start.1 = ((s8[8388608]{0:T(1024)(128)(4,1)}), s8[4194304]{0:T(1024)(128)(4,1)S(1)}, s32[]{:S(2)}) async-start(s8[8388608]{0:T(1024)(128)(4,1)} %bitcast.57), calls=%async_computation.2 | async-start | bytes 8388608
  263.3 48.0 %collective-permute-start.6 = (bf16[256,2048]{1,0:T(8,128)(2,1)S(1)}, bf16[256,2048]{1,0:T(8,128)(2,1)S(1)}, u32[]{:S(2)}, u32[]{:S(2)}) collective-permute-start(bf16[256,2048]{1,0:T(8,128)(2,1)S(1)} %pad_maximum_fusion.8), channel_id=1, source_target_pairs={{0,2},{2,0},{4,6},{6,4},{8,10},{10,8},{12,14},{14,12},{1,3},{3,1},... | collective-permute-start | bytes 3145736 | tf_op jit(solution)/shard_map/ppermute | solution.py:69
  312.0 25.6 %collective-permute-start.7 = (bf16[256,4096]{1,0:T(8,128)(2,1)S(1)}, bf16[256,4096]{1,0:T(8,128)(2,1)}, u32[]{:S(2)}, u32[]{:S(2)}) collective-permute-start(bf16[256,4096]{1,0:T(8,128)(2,1)S(1)} %select_dynamic-update-slice_fusion), channel_id=1, source_target_pairs={{0,16},{16,0},{1,17},{17,1},{2,18},{18,2},{3,19},{19,3},{4,20},{20... | collective-permute-start | bytes 6291464 | tf_op jit(solution)/shard_map/ppermute | solution.py:95
  313.3 24.1 %collective-permute-start.8 = (bf16[2,512,512]{2,1,0:T(8,128)(2,1)}, bf16[2,512,512]{2,1,0:T(8,128)(2,1)}, u32[]{:S(2)}, u32[]{:S(2)}) collective-permute-start(bf16[2,512,512]{2,1,0:T(8,128)(2,1)} %pad_maximum_fusion.9), channel_id=1, source_target_pairs={{0,1},{17,16},{2,3},{19,18},{4,5},{21,20},{6,7},{23,22},{8,9},{25,... | collective-permute-start | bytes 3145736 | tf_op jit(solution)/shard_map/ppermute | solution.py:91
  320.4 118.7 %collective-permute-start.9 = (bf16[4096,512]{1,0:T(8,128)(2,1)}, bf16[4096,512]{1,0:T(8,128)(2,1)}, u32[]{:S(2)}, u32[]{:S(2)}) collective-permute-start(bf16[4096,512]{1,0:T(8,128)(2,1)} %convert_element_type.93), channel_id=1, source_target_pairs={{0,1},{1,0},{2,3},{3,2},{4,5},{5,4},{6,7},{7,6},{8,9},{9,8},{10,11... | collective-permute-start | bytes 12582920 | tf_op jit(solution)/shard_map/ppermute | solution.py:22
  320.4 17.2 %copy-start.18 = (bf16[256,4096]{1,0:T(8,128)(2,1)S(1)}, bf16[256,4096]{1,0:T(8,128)(2,1)}, u32[]{:S(2)}) copy-start(bf16[256,4096]{1,0:T(8,128)(2,1)} %copy-done.17) | copy-start | bytes 6291460
  339.9 19.8 %copy-start.2 = (bf16[256,4096]{1,0:T(8,128)(2,1)}, bf16[256,4096]{1,0:T(8,128)(2,1)S(1)}, u32[]{:S(2)}) copy-start(bf16[256,4096]{1,0:T(8,128)(2,1)S(1)} %get-tuple-element.27) | copy-start | bytes 6291460
  345.4 85.0 %collective-permute-start.10 = (bf16[512,512]{1,0:T(8,128)(2,1)S(1)}, bf16[512,512]{1,0:T(8,128)(2,1)S(1)}, u32[]{:S(2)}, u32[]{:S(2)}) collective-permute-start(bf16[512,512]{1,0:T(8,128)(2,1)S(1)} %get-tuple-element.44), channel_id=1, source_target_pairs={{0,1},{1,0},{2,3},{3,2},{4,5},{5,4},{6,7},{7,6},{8,9},{9,8},{10,11... | collective-permute-start | bytes 1572872 | tf_op jit(solution)/shard_map/ppermute | solution.py:22
  430.7 16.7 %slice-start.2 = ((s8[8388608]{0:T(1024)(128)(4,1)}), s8[4194304]{0:T(1024)(128)(4,1)S(1)}, s32[]{:S(2)}) async-start(s8[8388608]{0:T(1024)(128)(4,1)} %bitcast.59), calls=%async_computation.3 | async-start | bytes 8388608
  430.7 16.7 %slice-start.6 = ((s8[8388608]{0:T(1024)(128)(4,1)}), s8[4194304]{0:T(1024)(128)(4,1)S(1)}, s32[]{:S(2)}) async-start(s8[8388608]{0:T(1024)(128)(4,1)} %bitcast.63), calls=%async_computation.7 | async-start | bytes 8388608
  449.6 137.6 %copy-start.7 = (f32[1024,512]{1,0:T(8,128)}, f32[1024,512]{1,0:T(8,128)S(1)}, u32[]{:S(2)}) copy-start(f32[1024,512]{1,0:T(8,128)S(1)} %get-tuple-element.51) | copy-start | bytes 6291460
  449.6 114.9 %collective-permute-start.12 = (bf16[1024,512]{1,0:T(8,128)(2,1)}, bf16[1024,512]{1,0:T(8,128)(2,1)}, u32[]{:S(2)}, u32[]{:S(2)}) collective-permute-start(bf16[1024,512]{1,0:T(8,128)(2,1)} %get-tuple-element.50), channel_id=1, source_target_pairs={{0,1},{1,0},{2,3},{3,2},{4,5},{5,4},{6,7},{7,6},{8,9},{9,8},{10,11... | collective-permute-start | bytes 3145736 | tf_op jit(solution)/shard_map/ppermute | solution.py:22
  474.3 91.5 %collective-permute-start.13 = (bf16[1024,512]{1,0:T(8,128)(2,1)}, bf16[1024,512]{1,0:T(8,128)(2,1)}, u32[]{:S(2)}, u32[]{:S(2)}) collective-permute-start(bf16[1024,512]{1,0:T(8,128)(2,1)} %get-tuple-element.48), channel_id=1, source_target_pairs={{0,1},{1,0},{2,3},{3,2},{4,5},{5,4},{6,7},{7,6},{8,9},{9,8},{10,11... | collective-permute-start | bytes 3145736 | tf_op jit(solution)/shard_map/ppermute | solution.py:22
  497.3 69.8 %collective-permute-start.14 = (bf16[1024,512]{1,0:T(8,128)(2,1)}, bf16[1024,512]{1,0:T(8,128)(2,1)}, u32[]{:S(2)}, u32[]{:S(2)}) collective-permute-start(bf16[1024,512]{1,0:T(8,128)(2,1)} %get-tuple-element.46), channel_id=1, source_target_pairs={{0,1},{1,0},{2,3},{3,2},{4,5},{5,4},{6,7},{7,6},{8,9},{9,8},{10,11... | collective-permute-start | bytes 3145736 | tf_op jit(solution)/shard_map/ppermute | solution.py:22
  523.3 53.6 %copy-start.11 = (f32[1024,512]{1,0:T(8,128)}, f32[1024,512]{1,0:T(8,128)S(1)}, u32[]{:S(2)}) copy-start(f32[1024,512]{1,0:T(8,128)S(1)} %get-tuple-element.53) | copy-start | bytes 6291460
  523.3 41.1 %collective-permute-start.11 = (bf16[1024,512]{1,0:T(8,128)(2,1)S(1)}, bf16[1024,512]{1,0:T(8,128)(2,1)S(1)}, u32[]{:S(2)}, u32[]{:S(2)}) collective-permute-start(bf16[1024,512]{1,0:T(8,128)(2,1)S(1)} %get-tuple-element.52), channel_id=1, source_target_pairs={{0,1},{1,0},{2,3},{3,2},{4,5},{5,4},{6,7},{7,6},{8,9},{9,8},{10,11... | collective-permute-start | bytes 3145736 | tf_op jit(solution)/shard_map/ppermute | solution.py:22
  524.9 39.3 %collective-permute-start.15 = (bf16[512,512]{1,0:T(8,128)(2,1)S(1)}, bf16[512,512]{1,0:T(8,128)(2,1)S(1)}, u32[]{:S(2)}, u32[]{:S(2)}) collective-permute-start(bf16[512,512]{1,0:T(8,128)(2,1)S(1)} %get-tuple-element.54), channel_id=1, source_target_pairs={{0,1},{1,0},{2,3},{3,2},{4,5},{5,4},{6,7},{7,6},{8,9},{9,8},{10,11... | collective-permute-start | bytes 1572872 | tf_op jit(solution)/shard_map/ppermute | solution.py:22
  612.1 24.6 %copy-start.8 = (f32[1024,512]{1,0:T(8,128)S(1)}, f32[1024,512]{1,0:T(8,128)}, u32[]{:S(2)}) copy-start(f32[1024,512]{1,0:T(8,128)} %copy-done.7) | copy-start | bytes 6291460
  618.4 1.1 collective-permute-start.16
  619.6 3.5 collective-permute-start.17
  623.2 3.5 collective-permute-start.18
  626.7 3.5 collective-permute-start.19
  630.3 4.4 collective-permute-start.20
  (25 other events, 199.6 us)
Sparse Core Ops, SparseCore 0:
  13.4 395.4 all-gather.1
where the time goes:
time: 666 us; the launch traced here: 658 us
  waiting for transfers between devices  368 us (55%)
  matrix products  195 us (29%)
  other arithmetic  40.3 us (6%)
  starting transfers between devices  25.8 us (4%)
  between operations  21.7 us (3%)
  local copies, waits for them, and re-layouts  7.34 us (1%)
    ppermute x3, waiting for transfers between devices, scatter_sum(): got = lax.ppermute(send, axis, [(i, i ^ bit) for i in range(n)]).astype(f32)  175 us
    dot_general x22, matrix products, dot(): return jnp.dot(a, b, preferred_element_type=f32)  161 us
    ppermute x3, waiting for transfers between devices, gather_columns(): got = lax.ppermute(own, axis, [(i, i ^ bit) for i in range(n)])  92.2 us
    ppermute x7, waiting for transfers between devices, shifted(): return lax.ppermute(block, axis, [(i, (i + shift) % n) for i in range(n)])  69 us
    dot_general x10, matrix products, token_inner(): lax.dot_general(left, right, (((0,), (0,)), ((), ())), preferred_element_...  33.4 us
    ppermute x1, waiting for transfers between devices, make_states(): away = lax.ppermute(pair, ('mp', 'tok'), [(0, 1), (3, 2)])  17.1 us
    sub x1, other arithmetic, per_device(): residual - step_size * jnp.concatenate(applied, 0)  14.1 us
  transfers between devices with their start and end apart: 22, of which 14 were waited for; matrix products, arithmetic and copies ran while one was open for 25% of the time, Pallas kernels for 0%

commit v1 on v0

--- a/solution.py
+++ b/solution.py
@@ -112,39 +112,57 @@
     step = height // CHUNKS
     cuts = [slice(c * step, (c + 1) * step) for c in range(CHUNKS)]
 
-    map_half = map_old.astype(bf16)
-    gram_old_half = gram_old.astype(bf16)
-    gram_old_half, context = lax.optimization_barrier((gram_old_half, context))
-    panel = lax.all_gather(gram_old_half, ("mp", "heads"), axis=1, tiled=True)
-    maps = [map_half] + [shifted(map_half, "tok", s) for s in range(1, n_tok)]
+    def by_owner(blocks):
+        if n_tok == 2:
+            own, other = blocks
+            return [jnp.where(t == 0, own, other), jnp.where(t == 0, other, own)]
+        stacked = jnp.stack(blocks)
+        return [
+            lax.dynamic_index_in_dim(stacked, lax.rem(t - o + n_tok, n_tok), 0, keepdims=False)
+            for o in range(n_tok)
+        ]
+
+    def all_shifts(block):
+        return [block] + [shifted(block, "tok", s) for s in range(1, n_tok)]
+
+    panels = [
+        lax.all_gather(gram_old[cut].astype(bf16), ("mp", "heads"), axis=1, tiled=True) for cut in cuts
+    ]
+    maps = by_owner(all_shifts(map_old.astype(bf16)))
     source, source_cols, target_cols = make_states(context, out_weight, skip_states, width)
-
     gram_new = decay_keep * gram_old + new_weight * token_inner(source, source_cols)
     cross_new = decay_keep * cross_old + new_weight * token_inner(source, target_cols)
+    inner_map = sum_tok(dot(source, map_old.astype(bf16)))
 
-    def panel_part(cut, s):
-        owner = lax.rem(t - s + n_tok, n_tok)
-        return lax.dynamic_slice(panel, (cut.start, owner * height), (step, height))
-
-    inner_map = sum_tok(dot(source, map_half))
-    residuals, halves = [], []
-    for cut in cuts:
-        product = sum(dot(panel_part(cut, s), maps[s]) for s in range(n_tok))
+    residuals, halves, inner_parts = [], [], []
+    strips = []
+    applied = [None] * CHUNKS
+    for r, cut in enumerate(cuts):
+        panel = panels[r]
+        product = sum(dot(panel[:, o * height:(o + 1) * height], maps[o]) for o in range(n_tok))
         low_rank = token_inner(source[:, cut], inner_map)
         residual = (
             cross_new[cut] - decay_keep * product - new_weight * low_rank - ridge_weight * map_old[cut]
         )
         residuals.append(residual)
-        halves.append(residual.astype(bf16))
-    away = [[shifted(half, "tok", s) for half in halves] for s in range(1, n_tok)]
-    inner_residual = sum_tok(sum(dot(source[:, cut], half) for cut, half in zip(cuts, halves)))
-    blocks = [jnp.concatenate(halves, 0)] + [jnp.concatenate(a, 0) for a in away]
-    applied, squares, mixed = [], 0.0, 0.0
-    for cut, residual in zip(cuts, residuals):
-        product = sum(dot(panel_part(cut, s), blocks[s]) for s in range(n_tok))
+        half = residual.astype(bf16)
+        inner_parts.append(dot(source[:, cut], half))
+        strips.append(by_owner(all_shifts(half)))
+        for i in range(r):
+            for o in range(n_tok):
+                begin = o * height + r * step
+                applied[i] = applied[i] + dot(panels[i][:, begin:begin + step], strips[r][o])
+        for o in range(n_tok):
+            known = strips[0][o] if r == 0 else jnp.concatenate([s[o] for s in strips], 0)
+            value = dot(panel[:, o * height:o * height + (r + 1) * step], known)
+            applied[r] = value if applied[r] is None else applied[r] + value
+    inner_residual = sum_tok(sum(inner_parts))
+    squares, mixed = 0.0, 0.0
+    values = []
+    for cut, residual, product in zip(cuts, residuals, applied):
         low_rank = token_inner(source[:, cut], inner_residual)
         value = decay_keep * product + new_weight * low_rank + ridge_weight * residual
-        applied.append(value)
+        values.append(value)
         squares = squares + jnp.sum(residual * residual)
         mixed = mixed + jnp.sum(residual * value)
     totals = jnp.stack([squares, mixed])
@@ -156,7 +174,7 @@
         gram_new,
         cross_new,
         map_old + step_size * residual,
-        residual - step_size * jnp.concatenate(applied, 0),
+        residual - step_size * jnp.concatenate(values, 0),
     )
 
 

time: 666 us -> 820 us (1.23)
  waiting for transfers between devices: 368 us -> 492 us
  other arithmetic: 40.3 us -> 55.3 us
  local copies, waits for them, and re-layouts: 7.34 us -> 15.7 us
    all_gather x1 -> x4, waiting for transfers between devices: 0.02 us -> 184 us  [per_device(): lax.all_gather(gram_old[cut].astype(bf16), ('mp', 'heads'), axis=1, tiled...]
    ppermute x3, waiting for transfers between devices: 175 us -> 151 us  [scatter_sum(): got = lax.ppermute(send, axis, [(i, i ^ bit) for i in range(n)]).astype(f32)]
    ppermute x7, waiting for transfers between devices: 69 us -> 50.1 us  [shifted(): return lax.ppermute(block, axis, [(i, (i + shift) % n) for i in range(n)])]
    ppermute x1, waiting for transfers between devices: 17.1 us -> 0.8 us  [make_states(): away = lax.ppermute(pair, ('mp', 'tok'), [(0, 1), (3, 2)])]
    select_n x0 -> x5, other arithmetic: none -> 15.4 us  [by_owner(): return [jnp.where(t == 0, own, other), jnp.where(t == 0, other, own)]]
    dot_general x10, matrix products: 33.4 us -> 42 us  [token_inner(): lax.dot_general(left, right, (((0,), (0,)), ((), ())), preferred_element_...]
    dot_general x22 -> x34, matrix products: 161 us -> 159 us  [dot(): return jnp.dot(a, b, preferred_element_type=f32)]
  transfers between devices with their start and end apart: 22 -> 25, of which waited for: 14 -> 19; matrix products, arithmetic and copies ran while one was open for 25% -> 18% of each run, Pallas kernels for 0% -> 0%
where the time goes in v1:
time: 820 us; the launch traced here: 812 us
  waiting for transfers between devices  492 us (60%)
  matrix products  201 us (25%)
  other arithmetic  55.3 us (7%)
  starting transfers between devices  25.6 us (3%)
  between operations  21.9 us (3%)
  local copies, waits for them, and re-layouts  15.7 us (2%)
    all_gather x4, waiting for transfers between devices, per_device(): lax.all_gather(gram_old[cut].astype(bf16), ('mp', 'heads'), axis=1, tiled...  184 us
    dot_general x34, matrix products, dot(): return jnp.dot(a, b, preferred_element_type=f32)  159 us
    ppermute x3, waiting for transfers between devices, scatter_sum(): got = lax.ppermute(send, axis, [(i, i ^ bit) for i in range(n)]).astype(f32)  151 us
    ppermute x3, waiting for transfers between devices, gather_columns(): got = lax.ppermute(own, axis, [(i, i ^ bit) for i in range(n)])  91.1 us
    ppermute x7, waiting for transfers between devices, shifted(): return lax.ppermute(block, axis, [(i, (i + shift) % n) for i in range(n)])  50.1 us
    dot_general x10, matrix products, token_inner(): lax.dot_general(left, right, (((0,), (0,)), ((), ())), preferred_element_...  42 us
  transfers between devices with their start and end apart: 25, of which 19 were waited for; matrix products, arithmetic and copies ran while one was open for 18% of the time, Pallas kernels for 0%

profile of v1, /device:TPU:0, one launch (start us, length us, event | category | flops | bytes accessed | tf_op | source)
XLA Modules:
  0.0 812.0 jit_solution(3079148440028956907)
XLA Ops:
  15.4 8.1 fusion.27
  30.1 60.0 %collective-permute-done = bf16[512,2048]{1,0:T(8,128)(2,1)S(1)} collective-permute-done((bf16[512,2048]{1,0:T(8,128)(2,1)}, bf16[512,2048]{1,0:T(8,128)(2,1)S(1)}, u32[]{:S(2)}, u32[]{:S(2)}) %collective-permute-start) | collective-permute-done | bytes 2097184 | tf_op jit(solution)/shard_map/ppermute | solution.py:55
  94.5 61.9 %collective-permute-done.1 = bf16[512,1024]{1,0:T(8,128)(2,1)S(1)} collective-permute-done((bf16[512,1024]{1,0:T(8,128)(2,1)S(1)}, bf16[512,1024]{1,0:T(8,128)(2,1)S(1)}, u32[]{:S(2)}, u32[]{:S(2)}) %collective-permute-start.1) | collective-permute-done | bytes 1048608 | tf_op jit(solution)/shard_map/ppermute | solution.py:55
  156.7 4.8 select_convert_fusion
  161.6 29.5 %collective-permute-done.2 = bf16[512,512]{1,0:T(8,128)(2,1)S(1)} collective-permute-done((bf16[512,512]{1,0:T(8,128)(2,1)S(1)}, bf16[512,512]{1,0:T(8,128)(2,1)S(1)}, u32[]{:S(2)}, u32[]{:S(2)}) %collective-permute-start.2) | collective-permute-done | bytes 524320 | tf_op jit(solution)/shard_map/ppermute | solution.py:55
  194.6 29.3 %collective-permute-done.4 = bf16[256,512]{1,0:T(8,128)(2,1)S(1)} collective-permute-done((bf16[256,512]{1,0:T(8,128)(2,1)S(1)}, bf16[256,512]{1,0:T(8,128)(2,1)S(1)}, u32[]{:S(2)}, u32[]{:S(2)}) %collective-permute-start.4) | collective-permute-done | bytes 262176 | tf_op jit(solution)/shard_map/ppermute | solution.py:69
  224.2 6.1 convert_element_type.94
  232.1 20.0 %collective-permute-done.5 = bf16[256,1024]{1,0:T(8,128)(2,1)S(1)} collective-permute-done((bf16[256,1024]{1,0:T(8,128)(2,1)S(1)}, bf16[256,1024]{1,0:T(8,128)(2,1)S(1)}, u32[]{:S(2)}, u32[]{:S(2)}) %collective-permute-start.5) | collective-permute-done | bytes 524320 | tf_op jit(solution)/shard_map/ppermute | solution.py:69
  254.0 41.8 %collective-permute-done.6 = bf16[256,2048]{1,0:T(8,128)(2,1)S(1)} collective-permute-done((bf16[256,2048]{1,0:T(8,128)(2,1)S(1)}, bf16[256,2048]{1,0:T(8,128)(2,1)S(1)}, u32[]{:S(2)}, u32[]{:S(2)}) %collective-permute-start.6) | collective-permute-done | bytes 1048608 | tf_op jit(solution)/shard_map/ppermute | solution.py:69
  300.3 23.8 %collective-permute-done.9 = bf16[4096,512]{1,0:T(8,128)(2,1)} collective-permute-done((bf16[4096,512]{1,0:T(8,128)(2,1)}, bf16[4096,512]{1,0:T(8,128)(2,1)}, u32[]{:S(2)}, u32[]{:S(2)}) %collective-permute-start.9) | collective-permute-done | bytes 4194336 | tf_op jit(solution)/shard_map/ppermute | solution.py:22
  324.0 8.6 %broadcast_select_fusion = (bf16[4096,512]{1,0:T(8,128)(2,1)}, bf16[4096,512]{1,0:T(8,128)(2,1)}) fusion(bf16[4096,512]{1,0:T(8,128)(2,1)} %collective-permute-done.9, pred[]{:T(512)S(6)} %eq.45, f32[4096,512]{1,0:T(8,128)} %param.11), kind=kLoop, calls=%fused_computation.60 | loop fusion | flops 6291456 | bytes 20971520 | tf_op jit(solution)/shard_map/jit(_where)/select_n | solution.py:118
  335.9 6.1 fusion.126
  344.6 5.0 multiply_add_fusion.1
  351.2 5.6 collective-permute-done.10
  357.1 8.3 %fusion.15 = f32[512,1024]{0,1:T(8,128)S(1)} fusion(bf16[4096,512]{1,0:T(8,128)(2,1)} %get-tuple-element.19, bf16[1024,8192]{1,0:T(8,128)(2,1)} %all-gather.11.cloned.1.call-done), kind=kOutput, calls=%fused_computation.20 | convolution fusion | flops 4294967296 | bytes 14680064 | tf_op jit(solution)/shard_map/dot_general | solution.py:13
  373.5 5.1 fusion.127
  378.8 8.9 %fusion = f32[512,1024]{0,1:T(8,128)S(1)} fusion(bf16[4096,512]{1,0:T(8,128)(2,1)} %get-tuple-element.19, bf16[1024,8192]{1,0:T(8,128)(2,1)} %all-gather.9.cloned.1.call-done), kind=kOutput, calls=%fused_computation | convolution fusion | flops 4294967296 | bytes 14680064 | tf_op jit(solution)/shard_map/dot_general | solution.py:13
  400.4 84.6 %all-gather.7.cloned.1.call-done = bf16[1024,8192]{1,0:T(8,128)(2,1)} async-done(((bf16[1024,512]{1,0:T(8,128)(2,1)}), bf16[1024,8192]{1,0:T(8,128)(2,1)}) %all-gather.7.cloned.1.call-update) | async-done | bytes 16777232 | tf_op jit(solution)/shard_map/all_gather | solution.py:129
  485.1 8.3 %fusion.4 = f32[512,1024]{0,1:T(8,128)S(1)} fusion(bf16[4096,512]{1,0:T(8,128)(2,1)} %get-tuple-element.19, bf16[1024,8192]{1,0:T(8,128)(2,1)} %all-gather.7.cloned.1.call-done), kind=kOutput, calls=%fused_computation.4 | convolution fusion | flops 4294967296 | bytes 14680064 | tf_op jit(solution)/shard_map/dot_general | solution.py:13
  501.3 5.1 fusion.129
  516.7 98.9 %all-gather.5.cloned.1.call-done = bf16[1024,8192]{1,0:T(8,128)(2,1)} async-done(((bf16[1024,512]{1,0:T(8,128)(2,1)}), bf16[1024,8192]{1,0:T(8,128)(2,1)}) %all-gather.5.cloned.1.call-update) | async-done | bytes 16777232 | tf_op jit(solution)/shard_map/all_gather | solution.py:129
  615.6 8.3 %fusion.8 = f32[512,1024]{0,1:T(8,128)S(1)} fusion(bf16[4096,512]{1,0:T(8,128)(2,1)} %get-tuple-element.19, bf16[1024,8192]{1,0:T(8,128)(2,1)} %all-gather.5.cloned.1.call-done), kind=kOutput, calls=%fused_computation.8 | convolution fusion | flops 4294967296 | bytes 14680064 | tf_op jit(solution)/shard_map/dot_general | solution.py:13
  623.9 7.0 fusion.10
  637.8 5.0 multiply_add_fusion.2
  644.3 5.9 collective-permute-done.15
  657.2 14.8 %collective-permute-done.11 = bf16[1024,512]{1,0:T(8,128)(2,1)S(1)} collective-permute-done((bf16[1024,512]{1,0:T(8,128)(2,1)S(1)}, bf16[1024,512]{1,0:T(8,128)(2,1)S(1)}, u32[]{:S(2)}, u32[]{:S(2)}) %collective-permute-start.11) | collective-permute-done | bytes 1048608 | tf_op jit(solution)/shard_map/ppermute | solution.py:22
  688.9 4.7 fusion.32
  726.4 7.2 fusion.23
  733.6 6.3 fusion.25
  750.0 9.4 %fusion.17 = f32[512,1024]{0,1:T(8,128)S(1)} fusion(bf16[1024,8192]{1,0:T(8,128)(2,1)} %all-gather.11.cloned.1.call-done, bf16[1024,512]{1,0:T(8,128)(2,1)} %copy-done.34, bf16[1024,512]{1,0:T(8,128)(2,1)} %copy-done.39, bf16[1024,512]{1,0:T(8,128)(2,1)} %copy-done.43, bf16[1024,512]{1,0:T(8,128)(2,1)} %copy-done.47), kind=kOutput, calls=%fused_computation.22 | convolution fusion | flops 4311744512 | bytes 14680064 | tf_op jit(solution)/shard_map/dot_general | solution.py:13
  759.4 8.0 fusion.21
  790.9 14.1 %fusion.12 = (f32[4096,512]{1,0:T(8,128)}, f32[4096,512]{1,0:T(8,128)}) fusion(f32[1024,512]{1,0:T(8,128)} %get-tuple-element.70, f32[1024,512]{1,0:T(8,128)} %get-tuple-element.69, f32[1024,512]{1,0:T(8,128)} %get-tuple-element.12, f32[1024,512]{1,0:T(8,128)} %get-tuple-element.13, f32[1024,512]{1,0:T(8,128)S(1)} %copy-done.5, f32[1024,512]{1,0:T(8,128)} %copy-done.6, ...), kind=kLoop, calls=%fused_computation.14 | loop fusion | flops 20971520 | bytes 41943044 | tf_op jit(solution)/shard_map/sub | solution.py:177
  (232 shorter events, 169.8 us)
Async XLA Ops:
  7.2 349.9 %all-gather.11.cloned.1.call-start = ((), (), s32[]{:S(2)}) async-start(), calls=%async_computation.3 | async-start | bytes 17825792 | tf_op jit(solution)/shard_map/all_gather | solution.py:129
  13.3 365.5 %all-gather.9.cloned.1.call-start = ((), (), s32[]{:S(2)}) async-start(), calls=%async_computation.2 | async-start | bytes 17825792 | tf_op jit(solution)/shard_map/all_gather | solution.py:129
  14.1 471.0 %all-gather.7.cloned.1.call-start = ((), (), s32[]{:S(2)}) async-start(), calls=%async_computation.1 | async-start | bytes 17825792 | tf_op jit(solution)/shard_map/all_gather | solution.py:129
  14.8 600.7 %all-gather.5.cloned.1.call-start = ((), (), s32[]{:S(2)}) async-start(), calls=%async_computation | async-start | bytes 17825792 | tf_op jit(solution)/shard_map/all_gather | solution.py:129
  27.2 63.0 %collective-permute-start = (bf16[512,2048]{1,0:T(8,128)(2,1)}, bf16[512,2048]{1,0:T(8,128)(2,1)S(1)}, u32[]{:S(2)}, u32[]{:S(2)}) collective-permute-start(bf16[512,2048]{1,0:T(8,128)(2,1)} %pad_maximum_fusion.2), channel_id=1, source_target_pairs={{0,2},{2,0},{4,6},{6,4},{8,10},{10,8},{12,14},{14,12},{1,3},{3,1},... | collective-permute-start | bytes 6291464 | tf_op jit(solution)/shard_map/ppermute | solution.py:55
  30.1 60.6 %copy-start.3 = (bf16[512,4096]{1,0:T(8,128)(2,1)S(1)}, bf16[512,4096]{1,0:T(8,128)(2,1)}, u32[]{:S(2)}) copy-start(bf16[512,4096]{1,0:T(8,128)(2,1)} %copy-done.2) | copy-start | bytes 12582916
  92.9 63.6 %collective-permute-start.1 = (bf16[512,1024]{1,0:T(8,128)(2,1)S(1)}, bf16[512,1024]{1,0:T(8,128)(2,1)S(1)}, u32[]{:S(2)}, u32[]{:S(2)}) collective-permute-start(bf16[512,1024]{1,0:T(8,128)(2,1)S(1)} %pad_maximum_fusion.6), channel_id=1, source_target_pairs={{0,4},{2,6},{4,0},{6,2},{8,12},{10,14},{12,8},{14,10},{1,5},{3,7},... | collective-permute-start | bytes 3145736 | tf_op jit(solution)/shard_map/ppermute | solution.py:55
  161.5 29.5 %collective-permute-start.2 = (bf16[512,512]{1,0:T(8,128)(2,1)S(1)}, bf16[512,512]{1,0:T(8,128)(2,1)S(1)}, u32[]{:S(2)}, u32[]{:S(2)}) collective-permute-start(bf16[512,512]{1,0:T(8,128)(2,1)S(1)} %get-tuple-element.14), channel_id=1, source_target_pairs={{0,8},{2,10},{4,12},{6,14},{8,0},{10,2},{12,4},{14,6},{1,9},{3,11}... | collective-permute-start | bytes 1572872 | tf_op jit(solution)/shard_map/ppermute | solution.py:55
  192.4 2.0 collective-permute-start.3
  194.5 29.4 %collective-permute-start.4 = (bf16[256,512]{1,0:T(8,128)(2,1)S(1)}, bf16[256,512]{1,0:T(8,128)(2,1)S(1)}, u32[]{:S(2)}, u32[]{:S(2)}) collective-permute-start(bf16[256,512]{1,0:T(8,128)(2,1)S(1)} %constant_dynamic-slice_fusion), channel_id=1, source_target_pairs={{0,8},{2,10},{4,12},{6,14},{8,0},{10,2},{12,4},{14,6},{1,9},{3,11}... | collective-permute-start | bytes 786440 | tf_op jit(solution)/shard_map/ppermute | solution.py:69
  224.1 27.9 %collective-permute-start.5 = (bf16[256,1024]{1,0:T(8,128)(2,1)S(1)}, bf16[256,1024]{1,0:T(8,128)(2,1)S(1)}, u32[]{:S(2)}, u32[]{:S(2)}) collective-permute-start(bf16[256,1024]{1,0:T(8,128)(2,1)S(1)} %pad_maximum_fusion.9), channel_id=1, source_target_pairs={{0,4},{2,6},{4,0},{6,2},{8,12},{10,14},{12,8},{14,10},{1,5},{3,7},... | collective-permute-start | bytes 1572872 | tf_op jit(solution)/shard_map/ppermute | solution.py:69
  230.3 93.8 %collective-permute-start.9 = (bf16[4096,512]{1,0:T(8,128)(2,1)}, bf16[4096,512]{1,0:T(8,128)(2,1)}, u32[]{:S(2)}, u32[]{:S(2)}) collective-permute-start(bf16[4096,512]{1,0:T(8,128)(2,1)} %convert_element_type.94), channel_id=1, source_target_pairs={{0,1},{1,0},{2,3},{3,2},{4,5},{5,4},{6,7},{7,6},{8,9},{9,8},{10,11... | collective-permute-start | bytes 12582920 | tf_op jit(solution)/shard_map/ppermute | solution.py:22
  252.3 43.5 %collective-permute-start.6 = (bf16[256,2048]{1,0:T(8,128)(2,1)S(1)}, bf16[256,2048]{1,0:T(8,128)(2,1)S(1)}, u32[]{:S(2)}, u32[]{:S(2)}) collective-permute-start(bf16[256,2048]{1,0:T(8,128)(2,1)S(1)} %pad_maximum_fusion.7), channel_id=1, source_target_pairs={{0,2},{2,0},{4,6},{6,4},{8,10},{10,8},{12,14},{14,12},{1,3},{3,1},... | collective-permute-start | bytes 3145736 | tf_op jit(solution)/shard_map/ppermute | solution.py:69
  296.6 37.0 %collective-permute-start.7 = (bf16[256,4096]{1,0:T(8,128)(2,1)S(1)}, bf16[256,4096]{1,0:T(8,128)(2,1)}, u32[]{:S(2)}, u32[]{:S(2)}) collective-permute-start(bf16[256,4096]{1,0:T(8,128)(2,1)S(1)} %select_dynamic-update-slice_fusion), channel_id=1, source_target_pairs={{0,16},{16,0},{1,17},{17,1},{2,18},{18,2},{3,19},{19,3},{4,20},{20... | collective-permute-start | bytes 6291464 | tf_op jit(solution)/shard_map/ppermute | solution.py:95
  296.8 36.6 %collective-permute-start.8 = (bf16[2,512,512]{2,1,0:T(8,128)(2,1)S(1)}, bf16[2,512,512]{2,1,0:T(8,128)(2,1)S(1)}, u32[]{:S(2)}, u32[]{:S(2)}) collective-permute-start(bf16[2,512,512]{2,1,0:T(8,128)(2,1)S(1)} %pad_maximum_fusion.8), channel_id=1, source_target_pairs={{0,1},{17,16},{2,3},{19,18},{4,5},{21,20},{6,7},{23,22},{8,9},{25,... | collective-permute-start | bytes 3145736 | tf_op jit(solution)/shard_map/ppermute | solution.py:91
  342.0 14.8 %collective-permute-start.10 = (bf16[512,512]{1,0:T(8,128)(2,1)S(1)}, bf16[512,512]{1,0:T(8,128)(2,1)S(1)}, u32[]{:S(2)}, u32[]{:S(2)}) collective-permute-start(bf16[512,512]{1,0:T(8,128)(2,1)S(1)} %get-tuple-element.57), channel_id=1, source_target_pairs={{0,1},{1,0},{2,3},{3,2},{4,5},{5,4},{6,7},{7,6},{8,9},{9,8},{10,11... | collective-permute-start | bytes 1572872 | tf_op jit(solution)/shard_map/ppermute | solution.py:22
  378.6 271.8 %collective-permute-start.14 = (bf16[1024,512]{1,0:T(8,128)(2,1)}, bf16[1024,512]{1,0:T(8,128)(2,1)}, u32[]{:S(2)}, u32[]{:S(2)}) collective-permute-start(bf16[1024,512]{1,0:T(8,128)(2,1)} %get-tuple-element.59), channel_id=1, source_target_pairs={{0,1},{1,0},{2,3},{3,2},{4,5},{5,4},{6,7},{7,6},{8,9},{9,8},{10,11... | collective-permute-start | bytes 3145736 | tf_op jit(solution)/shard_map/ppermute | solution.py:22
  398.7 347.2 %copy-start.6 = (f32[1024,512]{1,0:T(8,128)}, f32[1024,512]{1,0:T(8,128)S(1)}, u32[]{:S(2)}) copy-start(f32[1024,512]{1,0:T(8,128)S(1)} %get-tuple-element.62) | copy-start | bytes 6291460
  398.7 253.6 %collective-permute-start.13 = (bf16[1024,512]{1,0:T(8,128)(2,1)}, bf16[1024,512]{1,0:T(8,128)(2,1)}, u32[]{:S(2)}, u32[]{:S(2)}) collective-permute-start(bf16[1024,512]{1,0:T(8,128)(2,1)} %get-tuple-element.61), channel_id=1, source_target_pairs={{0,1},{1,0},{2,3},{3,2},{4,5},{5,4},{6,7},{7,6},{8,9},{9,8},{10,11... | collective-permute-start | bytes 3145736 | tf_op jit(solution)/shard_map/ppermute | solution.py:22
  506.4 148.4 %collective-permute-start.12 = (bf16[1024,512]{1,0:T(8,128)(2,1)}, bf16[1024,512]{1,0:T(8,128)(2,1)}, u32[]{:S(2)}, u32[]{:S(2)}) collective-permute-start(bf16[1024,512]{1,0:T(8,128)(2,1)} %get-tuple-element.63), channel_id=1, source_target_pairs={{0,1},{1,0},{2,3},{3,2},{4,5},{5,4},{6,7},{7,6},{8,9},{9,8},{10,11... | collective-permute-start | bytes 3145736 | tf_op jit(solution)/shard_map/ppermute | solution.py:22
  634.6 85.6 %copy-start.8 = (f32[1024,512]{1,0:T(8,128)}, f32[1024,512]{1,0:T(8,128)S(1)}, u32[]{:S(2)}) copy-start(f32[1024,512]{1,0:T(8,128)S(1)} %get-tuple-element.66) | copy-start | bytes 6291460
  635.4 14.8 %collective-permute-start.15 = (bf16[512,512]{1,0:T(8,128)(2,1)S(1)}, bf16[512,512]{1,0:T(8,128)(2,1)S(1)}, u32[]{:S(2)}, u32[]{:S(2)}) collective-permute-start(bf16[512,512]{1,0:T(8,128)(2,1)S(1)} %get-tuple-element.67), channel_id=1, source_target_pairs={{0,1},{1,0},{2,3},{3,2},{4,5},{5,4},{6,7},{7,6},{8,9},{9,8},{10,11... | collective-permute-start | bytes 1572872 | tf_op jit(solution)/shard_map/ppermute | solution.py:22
  642.8 29.2 %collective-permute-start.11 = (bf16[1024,512]{1,0:T(8,128)(2,1)S(1)}, bf16[1024,512]{1,0:T(8,128)(2,1)S(1)}, u32[]{:S(2)}, u32[]{:S(2)}) collective-permute-start(bf16[1024,512]{1,0:T(8,128)(2,1)S(1)} %get-tuple-element.65), channel_id=1, source_target_pairs={{0,1},{1,0},{2,3},{3,2},{4,5},{5,4},{6,7},{7,6},{8,9},{9,8},{10,11... | collective-permute-start | bytes 3145736 | tf_op jit(solution)/shard_map/ppermute | solution.py:22
  650.4 69.7 %copy-start.9 = (bf16[512,512]{1,0:T(8,128)(2,1)}, bf16[512,512]{1,0:T(8,128)(2,1)S(1)}, u32[]{:S(2)}) copy-start(bf16[512,512]{1,0:T(8,128)(2,1)S(1)} %add_convert_fusion) | copy-start | bytes 1572868
  652.3 62.1 %copy-start.31 = (bf16[1024,512]{1,0:T(8,128)(2,1)}, bf16[1024,512]{1,0:T(8,128)(2,1)S(1)}, u32[]{:S(2)}) copy-start(bf16[1024,512]{1,0:T(8,128)(2,1)S(1)} %get-tuple-element.43) | copy-start | bytes 3145732
  652.3 65.0 %copy-start.34 = (bf16[1024,512]{1,0:T(8,128)(2,1)}, bf16[1024,512]{1,0:T(8,128)(2,1)S(1)}, u32[]{:S(2)}) copy-start(bf16[1024,512]{1,0:T(8,128)(2,1)S(1)} %get-tuple-element.44) | copy-start | bytes 3145732
  654.8 56.8 %copy-start.39 = (bf16[1024,512]{1,0:T(8,128)(2,1)}, bf16[1024,512]{1,0:T(8,128)(2,1)S(1)}, u32[]{:S(2)}) copy-start(bf16[1024,512]{1,0:T(8,128)(2,1)S(1)} %get-tuple-element.42) | copy-start | bytes 3145732
  772.7 1.1 collective-permute-start.16
  773.9 3.5 collective-permute-start.17
  777.5 3.5 collective-permute-start.18
  781.0 3.5 collective-permute-start.19
  784.6 4.4 collective-permute-start.20
  (53 other events, 581.6 us)
Sparse Core Ops, SparseCore 0:
  13.5 175.1 all-gather.10
  190.7 161.5 all-gather.8
  354.4 130.6 all-gather.6
  487.0 128.5 all-gather.4

commit v2 on v0

--- a/solution.py
+++ b/solution.py
@@ -1,6 +1,8 @@
 import jax
 import jax.numpy as jnp
 from jax import lax
+from jax.experimental import pallas as pl
+from jax.experimental.pallas import tpu as pltpu
 from jax.sharding import PartitionSpec as P
 
 decay_keep = 0.75
@@ -160,9 +162,299 @@
     )
 
 
+UNITS = 16
+LATER = 48
+MESH = pl.DeviceIdType.MESH
+
+
+def gather_kernel(
+    g_ref, m_hbm, base_hbm, panel, res_hbm, app_hbm,
+    maps, rf, acc, prod, buf, col, base, own_sem, in_sem, col_sem, out_sem, zs, zr, ys, yr, bs, br, cs, cr, xs, xr,
+):
+    k, h, t = lax.axis_index("mp"), lax.axis_index("heads"), lax.axis_index("tok")
+    z, y = h // 2, h % 2
+    height, width = g_ref.shape
+    unit = height // UNITS
+    early = unit - LATER
+    chunks = rf.shape[0] // 2
+    step = height // chunks
+    steps = ((1, 0), (-1, 1))
+
+    def block(zz, yy):
+        return k * 8 + zz * 2 + yy
+
+    def inside(zz):
+        return (zz >= 0) & (zz <= 3)
+
+    def piece(zz, yy, u, lo, n):
+        return panel.at[block(zz, yy), pl.ds(pl.multiple_of(u * unit, unit) + lo, n)]
+
+    def remote(ref, send, recv, dev):
+        return pltpu.make_async_remote_copy(
+            src_ref=ref, dst_ref=ref, send_sem=send, recv_sem=recv, device_id=dev, device_id_type=MESH
+        )
+
+    def at_z(dz):
+        return (k, jnp.clip(z + dz, 0, 3) * 2 + y, t)
+
+    at_y = (k, z * 2 + 1 - y, t)
+    at_core = (1 - k, h, t)
+    at_x = (k, h, 1 - t)
+
+    def z_copy(s, dz, d, zz, u):
+        return remote(piece(jnp.clip(zz, 0, 3), y, u, 0, unit), zs.at[d, s, u], zr.at[d, s, u], at_z(dz))
+
+    def b_copy(s, dz, d, zz, u):
+        return remote(
+            piece(jnp.clip(zz, 0, 3), 1 - y, u, early, LATER), bs.at[d, s, u], br.at[d, s, u], at_z(dz)
+        )
+
+    def y_copy(zz, yy, u, n):
+        zz = jnp.clip(zz, 0, 3)
+        return remote(piece(zz, yy, u, 0, n), ys.at[zz, u], yr.at[zz, u], at_y)
+
+    def core_copy(kk, u):
+        ref = panel.at[pl.ds(kk * 8, 8), pl.ds(pl.multiple_of(u * unit, unit), unit)]
+        return remote(ref, cs.at[u], cr.at[u], at_core)
+
+    def x_copy(tt, c):
+        return remote(rf.at[tt * chunks + c], xs.at[c], xr.at[c], at_x)
+
+    own = pltpu.make_async_copy(g_ref, panel.at[block(z, y)], own_sem)
+    own.start()
+    load_maps = pltpu.make_async_copy(m_hbm, maps, in_sem)
+    load_maps.start()
+    barrier = pltpu.get_barrier_semaphore()
+    for dev in (at_y, at_core, at_x):
+        pl.semaphore_signal(barrier, inc=1, device_id=dev, device_id_type=MESH)
+    for dz, d in steps:
+        @pl.when(inside(z + dz))
+        def _():
+            pl.semaphore_signal(barrier, inc=1, device_id=at_z(dz), device_id_type=MESH)
+    pl.semaphore_wait(barrier, 3 + jnp.where(z > 0, 1, 0) + jnp.where(z < 3, 1, 0))
+    own.wait()
+    load_maps.wait()
+
+    def valid(u):
+        return (u >= 0) & (u < UNITS)
+
+    def product_one(c):
+        for half in range(2):
+            core_copy(1 - k, 2 * c + half).wait_recv()
+        rows = pl.ds(pl.multiple_of(c * step, step), step)
+        load = pltpu.make_async_copy(panel.at[:, rows], buf, in_sem)
+        load.start()
+        load_base = pltpu.make_async_copy(base_hbm.at[rows], base, own_sem)
+        load_base.start()
+        load.wait()
+        prod[...] = jnp.zeros_like(prod)
+
+        @pl.loop(0, 8)
+        def _(q):
+            prod[...] += jnp.dot(buf[2 * q], maps[2 * q], preferred_element_type=f32) + jnp.dot(
+                buf[2 * q + 1], maps[2 * q + 1], preferred_element_type=f32
+            )
+
+        load_base.wait()
+        base[...] = base[...] - decay_keep * prod[...]
+        rf[t * chunks + c] = base[...].astype(bf16)
+        x_copy(t, c).start()
+        save = pltpu.make_async_copy(base, res_hbm.at[rows], out_sem)
+        save.start()
+        prod[...] = jnp.zeros_like(prod)
+
+        @pl.loop(0, c)
+        def _(i):
+            prod[...] += jnp.dot(buf[i], rf[i], preferred_element_type=f32) + jnp.dot(
+                buf[chunks + i], rf[chunks + i], preferred_element_type=f32
+            )
+
+        acc[c] = prod[...]
+        save.wait()
+
+    def column(c, i, slot, o):
+        return pltpu.make_async_copy(
+            panel.at[o * chunks + c, pl.ds(pl.multiple_of(i * step, step), step)],
+            col.at[slot, o],
+            col_sem.at[slot, o],
+        )
+
+    def product_two(c):
+        for o in range(2):
+            column(c, 0, 0, o).start()
+        x_copy(1 - t, c).wait_recv()
+
+        @pl.loop(0, c + 1)
+        def _(i):
+            slot = i % 2
+
+            @pl.when(i < c)
+            def _():
+                for o in range(2):
+                    column(c, i + 1, 1 - slot, o).start()
+
+            for o in range(2):
+                column(c, i, slot, o).wait()
+            acc[i] += jnp.dot(col[slot, 0], rf[c], preferred_element_type=f32) + jnp.dot(
+                col[slot, 1], rf[chunks + c], preferred_element_type=f32
+            )
+
+    @pl.loop(0, UNITS + 6)
+    def _(tick):
+        u0 = tick
+
+        @pl.when(u0 < UNITS)
+        def _():
+            for dz, d in steps:
+                @pl.when(inside(z + dz))
+                def _():
+                    z_copy(0, dz, d, z, u0).start()
+            y_copy(z, y, u0, unit).start()
+
+        for lag in range(1, 5):
+            u = tick - lag
+
+            @pl.when(valid(u))
+            def _():
+                if lag <= 3:
+                    for dz, d in steps:
+                        zz = z - lag * dz
+
+                        @pl.when(inside(zz))
+                        def _():
+                            z_copy(lag - 1, dz, d, zz, u).wait_recv()
+                            if lag < 3:
+                                @pl.when(inside(z + dz))
+                                def _():
+                                    z_copy(lag, dz, d, zz, u).start()
+                            y_copy(zz, y, u, early).start()
+                if lag == 1:
+                    y_copy(z, 1 - y, u, unit).wait_recv()
+                    for dz, d in steps:
+                        @pl.when(inside(z + dz))
+                        def _():
+                            b_copy(0, dz, d, z, u).start()
+                else:
+                    for dz, d in steps:
+                        zz = z - (lag - 1) * dz
+
+                        @pl.when(inside(zz))
+                        def _():
+                            y_copy(zz, 1 - y, u, early).wait_recv()
+                            b_copy(lag - 2, dz, d, zz, u).wait_recv()
+                            if lag < 4:
+                                @pl.when(inside(z + dz))
+                                def _():
+                                    b_copy(lag - 1, dz, d, zz, u).start()
+                if lag == 4:
+                    core_copy(k, u).start()
+
+        w = tick - 6
+
+        @pl.when((w >= 0) & (w % 2 == 0))
+        def _():
+            product_one(w // 2)
+
+        @pl.when((w >= 0) & (w % 2 == 1))
+        def _():
+            product_two(w // 2)
+
+    save = pltpu.make_async_copy(acc, app_hbm, out_sem)
+    save.start()
+
+    @pl.loop(0, UNITS)
+    def _(u):
+        for s in range(3):
+            for dz, d in steps:
+                @pl.when(inside(z - s * dz) & inside(z + dz))
+                def _():
+                    z_copy(s, dz, d, z - s * dz, u).wait_send()
+                    b_copy(s, dz, d, z - s * dz, u).wait_send()
+        y_copy(z, y, u, unit).wait_send()
+        for s in range(1, 4):
+            for dz, d in steps:
+                @pl.when(inside(z - s * dz))
+                def _():
+                    y_copy(z - s * dz, y, u, early).wait_send()
+        core_copy(k, u).wait_send()
+
+    @pl.loop(0, chunks)
+    def _(c):
+        x_copy(t, c).wait_send()
+
+    save.wait()
+
+
+def gather_and_multiply(gram_half, maps, base):
+    height, width = gram_half.shape
+    chunks = 8
+    step = height // chunks
+    any_space = pl.BlockSpec(memory_space=pltpu.HBM)
+    dma = pltpu.SemaphoreType.DMA
+    panel, residual, applied = pl.pallas_call(
+        gather_kernel,
+        out_shape=[
+            jax.ShapeDtypeStruct((16, height, width), bf16),
+            jax.ShapeDtypeStruct((height, width), f32),
+            jax.ShapeDtypeStruct((chunks, step, width), f32),
+        ],
+        in_specs=[any_space] * 3,
+        out_specs=[any_space] * 3,
+        scratch_shapes=[
+            pltpu.VMEM((16, step, width), bf16),
+            pltpu.VMEM((16, step, width), bf16),
+            pltpu.VMEM((chunks, step, width), f32),
+            pltpu.VMEM((step, width), f32),
+            pltpu.VMEM((16, step, width), bf16),
+            pltpu.VMEM((2, 2, step, width), bf16),
+            pltpu.VMEM((step, width), f32),
+            dma, dma, dma((2, 2)), dma,
+            dma((2, 3, UNITS)), dma((2, 3, UNITS)),
+            dma((4, UNITS)), dma((4, UNITS)),
+            dma((2, 3, UNITS)), dma((2, 3, UNITS)),
+            dma((UNITS,)), dma((UNITS,)),
+            dma((chunks,)), dma((chunks,)),
+        ],
+        compiler_params=pltpu.CompilerParams(
+            collective_id=0, has_side_effects=True, vmem_limit_bytes=56 * 1024 * 1024
+        ),
+        cost_estimate=pl.CostEstimate(
+            flops=4 * height * width * 16 * width, bytes_accessed=16 * height * width * 6, transcendentals=0
+        ),
+    )(gram_half, maps.reshape(16, step, width), base)
+    return residual, applied.reshape(height, width)
+
+
+def with_kernel(context, out_weight, skip_states, gram_old, cross_old, map_old):
+    t = lax.axis_index("tok")
+    tokens = context.shape[1]
+    width = gram_old.shape[1]
+    new_weight = (1.0 - decay_keep) / tokens
+    map_half = map_old.astype(bf16)
+    map_away = shifted(map_half, "tok", 1)
+    maps = jnp.concatenate(
+        [jnp.where(t == 0, map_half, map_away), jnp.where(t == 0, map_away, map_half)], 0
+    )
+    source, source_cols, target_cols = make_states(context, out_weight, skip_states, width)
+    inner_map = sum_tok(dot(source, map_half))
+    cross_new = decay_keep * cross_old + new_weight * token_inner(source, target_cols)
+    base = cross_new - new_weight * token_inner(source, inner_map) - ridge_weight * map_old
+    residual, product = gather_and_multiply(gram_old.astype(bf16), maps, base)
+    gram_new = decay_keep * gram_old + new_weight * token_inner(source, source_cols)
+    inner_residual = sum_tok(dot(source, residual.astype(bf16)))
+    applied = decay_keep * product + new_weight * token_inner(source, inner_residual) + ridge_weight * residual
+    totals = jnp.stack([jnp.sum(residual * residual), jnp.sum(residual * applied)])
+    for axis in ("mp", "tok", "heads"):
+        totals = total_over(totals, axis)
+    step_size = totals[0] / totals[1]
+    return gram_new, cross_new, map_old + step_size * residual, residual - step_size * applied
+
+
 def solution(mesh):
     block = P("tok", ("mp", "heads"))
     placed = (P("mp", None, "heads"), P("mp", "heads", "tok"), P(None, None, "tok"), block, block, block)
+    lines = dict(mesh.shape) == {"mp": 2, "heads": 8, "tok": 2}
     return jax.shard_map(
-        per_device, mesh=mesh, in_specs=placed, out_specs=(block,) * 4, check_vma=False
+        with_kernel if lines else per_device,
+        mesh=mesh, in_specs=placed, out_specs=(block,) * 4, check_vma=False,
     )

time: 666 us -> 847 us (1.27)
  Pallas kernels: 0 us -> 514 us
  waiting for transfers between devices: 368 us -> 184 us
  matrix products: 195 us -> 57.2 us
  other arithmetic: 40.3 us -> 68.1 us
  between operations: 21.7 us -> 2.35 us
  starting transfers between devices: 25.8 us -> 17.1 us
    pallas_call x0 -> x1, Pallas kernels: none -> 514 us  [gather_and_multiply(): pl.pallas_call(gather_kernel, out_shape=[jax.ShapeDtypeStruct((16, height...]
    dot_general x22 -> x3, matrix products: 161 us -> 21 us  [dot(): return jnp.dot(a, b, preferred_element_type=f32)]
    ppermute x3, waiting for transfers between devices: 175 us -> 90.2 us  [scatter_sum(): got = lax.ppermute(send, axis, [(i, i ^ bit) for i in range(n)]).astype(f32)]
    ppermute x3, waiting for transfers between devices: 92.2 us -> 33.2 us  [gather_columns(): got = lax.ppermute(own, axis, [(i, i ^ bit) for i in range(n)])]
    ppermute x7 -> x3, waiting for transfers between devices: 69 us -> 44 us  [shifted(): return lax.ppermute(block, axis, [(i, (i + shift) % n) for i in range(n)])]
    ppermute x1, waiting for transfers between devices: 17.1 us -> 0.01 us  [make_states(): away = lax.ppermute(pair, ('mp', 'tok'), [(0, 1), (3, 2)])]
    dot_general x10 -> x4, matrix products: 33.4 us -> 36.2 us  [token_inner(): lax.dot_general(left, right, (((0,), (0,)), ((), ())), preferred_element_...]
  transfers between devices with their start and end apart: 22 -> 17, of which waited for: 14 -> 14; matrix products, arithmetic and copies ran while one was open for 25% -> 6% of each run, Pallas kernels for 0% -> 0%
where the time goes in v2:
time: 847 us; the launch traced here: 845 us
  Pallas kernels  514 us (61%)
  waiting for transfers between devices  184 us (22%)
  other arithmetic  68.1 us (8%)
  matrix products  57.2 us (7%)
  starting transfers between devices  17.1 us (2%)
    pallas_call x1, Pallas kernels, gather_and_multiply(): pl.pallas_call(gather_kernel, out_shape=[jax.ShapeDtypeStruct((16, height...  514 us
    ppermute x3, waiting for transfers between devices, scatter_sum(): got = lax.ppermute(send, axis, [(i, i ^ bit) for i in range(n)]).astype(f32)  90.2 us
    ppermute x3, waiting for transfers between devices, shifted(): return lax.ppermute(block, axis, [(i, (i + shift) % n) for i in range(n)])  44 us
    dot_general x4, matrix products, token_inner(): lax.dot_general(left, right, (((0,), (0,)), ((), ())), preferred_element_...  36.2 us
    ppermute x3, waiting for transfers between devices, gather_columns(): got = lax.ppermute(own, axis, [(i, i ^ bit) for i in range(n)])  33.2 us
    dot_general x3, matrix products, dot(): return jnp.dot(a, b, preferred_element_type=f32)  21 us
  transfers between devices with their start and end apart: 17, of which 14 were waited for; matrix products, arithmetic and copies ran while one was open for 6% of the time, Pallas kernels for 0%

profile of v2, /device:TPU:0, one launch (start us, length us, event | category | flops | bytes accessed | tf_op | source)
XLA Modules:
  0.0 845.4 jit_solution(4318675533555147804)
XLA Ops:
  1.9 8.1 fusion.3
  10.2 2.0 pad_maximum_fusion.2
  12.6 3.0 collective-permute-start
  15.6 45.8 %collective-permute-done = bf16[512,2048]{1,0:T(8,128)(2,1)S(1)} collective-permute-done((bf16[512,2048]{1,0:T(8,128)(2,1)}, bf16[512,2048]{1,0:T(8,128)(2,1)S(1)}, u32[]{:S(2)}, u32[]{:S(2)}) %collective-permute-start) | collective-permute-done | bytes 2097184 | tf_op jit(solution)/shard_map/ppermute | solution.py:57
  66.0 22.5 %collective-permute-done.1 = bf16[512,1024]{1,0:T(8,128)(2,1)S(1)} collective-permute-done((bf16[512,1024]{1,0:T(8,128)(2,1)S(1)}, bf16[512,1024]{1,0:T(8,128)(2,1)S(1)}, u32[]{:S(2)}, u32[]{:S(2)}) %collective-permute-start.1) | collective-permute-done | bytes 1048608 | tf_op jit(solution)/shard_map/ppermute | solution.py:57
  88.8 4.6 select_convert_fusion
  93.4 2.6 collective-permute-start.2
  95.9 21.8 %collective-permute-done.2 = bf16[512,512]{1,0:T(8,128)(2,1)S(1)} collective-permute-done((bf16[512,512]{1,0:T(8,128)(2,1)S(1)}, bf16[512,512]{1,0:T(8,128)(2,1)S(1)}, u32[]{:S(2)}, u32[]{:S(2)}) %collective-permute-start.2) | collective-permute-done | bytes 524320 | tf_op jit(solution)/shard_map/ppermute | solution.py:57
  121.3 5.9 convert_element_type.84
  128.3 7.8 collective-permute-done.4
  136.4 13.4 %collective-permute-done.5 = bf16[256,1024]{1,0:T(8,128)(2,1)S(1)} collective-permute-done((bf16[256,1024]{1,0:T(8,128)(2,1)S(1)}, bf16[256,1024]{1,0:T(8,128)(2,1)S(1)}, u32[]{:S(2)}, u32[]{:S(2)}) %collective-permute-start.5) | collective-permute-done | bytes 524320 | tf_op jit(solution)/shard_map/ppermute | solution.py:71
  151.9 5.9 convert_element_type.83.g_ref
  158.8 4.4 collective-permute-start.8
  163.2 11.9 %collective-permute-done.6 = bf16[256,2048]{1,0:T(8,128)(2,1)S(1)} collective-permute-done((bf16[256,2048]{1,0:T(8,128)(2,1)}, bf16[256,2048]{1,0:T(8,128)(2,1)S(1)}, u32[]{:S(2)}, u32[]{:S(2)}) %collective-permute-start.6) | collective-permute-done | bytes 1048608 | tf_op jit(solution)/shard_map/ppermute | solution.py:71
  181.7 39.3 %collective-permute-done.9 = bf16[4096,512]{1,0:T(8,128)(2,1)} collective-permute-done((bf16[4096,512]{1,0:T(8,128)(2,1)}, bf16[4096,512]{1,0:T(8,128)(2,1)}, u32[]{:S(2)}, u32[]{:S(2)}) %collective-permute-start.9) | collective-permute-done | bytes 4194336 | tf_op jit(solution)/shard_map/ppermute | solution.py:24
  221.0 8.1 broadcast_select_fusion.1
  229.1 7.4 pad_maximum_fusion
  236.6 2.0 broadcast_select_fusion.3
  238.7 6.1 fusion.12
  246.3 4.9 multiply_add_fusion.2
  251.2 7.6 multiply_add_fusion.1
  258.9 12.4 %multiply_subtract_fusion.1.base_hbm = f32[4096,512]{1,0:T(8,128)} fusion(f32[4096,512]{1,0:T(8,128)S(1)} %bitcast.30, f32[4096,512]{1,0:T(8,128)S(1)} %multiply_add_fusion.1, f32[512,512]{1,0:T(8,128)S(1)} %get-tuple-element.38, bf16[512,512]{1,0:T(8,128)(2,1)S(1)} %collective-permute-done.10, bf16[256,4096]{1,0:T(8,128)(2,1)} %copy-done.8, ...), kind=kOutput, calls=%fused_computation.9 | convolution fusion | flops 2165047296 | bytes 30932992 | tf_op jit(solution)/shard_map/dot_general | solution.py:19
  271.3 513.6 %shard_map.93 = (bf16[16,4096,512]{2,1,0:T(8,128)(2,1)}, f32[4096,512]{1,0:T(8,128)}, f32[8,512,512]{2,1,0:T(8,128)}) custom-call(bf16[4096,512]{1,0:T(8,128)(2,1)} %convert_element_type.83.g_ref, bf16[16,512,512]{2,1,0:T(8,128)(2,1)} %bitcast.35, f32[4096,512]{1,0:T(8,128)} %multiply_subtract_fusion.1.base_hbm), custom_call_target="tpu_custom_call" | custom-call | flops 68719476736 | bytes 201326592 | tf_op jit(solution)/shard_map/pallas_call | solution.py:394
  785.0 6.8 fusion.13
  791.8 4.5 broadcast_multiply_fusion
  796.3 4.7 collective-permute-done.11
  801.0 11.3 %multiply_reduce_fusion.1 = (f32[]{:T(128)}, f32[]{:T(128)}, f32[4096,512]{1,0:T(8,128)}) fusion(f32[4096,512]{1,0:T(8,128)} %get-tuple-element.6, f32[512,512]{1,0:T(8,128)} %get-tuple-element.40, bf16[512,512]{1,0:T(8,128)(2,1)S(1)} %collective-permute-done.11, bf16[256,4096]{1,0:T(8,128)(2,1)S(1)} %copy-done.9, bf16[256,4096]{1,0:T(8,128)(2,1)S(1)} %copy-done.7, ...), kind=kOutput, calls=%fused_computation.8 | convolution fusion | flops 2173435904 | bytes 30933000 | tf_op jit(solution)/shard_map/dot_general | solution.py:19
  816.0 3.5 collective-permute-done.13
  822.4 1.9 collective-permute-done.14
  824.4 3.5 collective-permute-done.15
  827.9 4.4 collective-permute-done.16
  834.3 11.1 %multiply_subtract_fusion = (f32[4096,512]{1,0:T(8,128)}, f32[4096,512]{1,0:T(8,128)}) fusion(f32[4096,512]{1,0:T(8,128)} %get-tuple-element.6, f32[4096,512]{1,0:T(8,128)} %get-tuple-element.41, f32[]{:T(128)} %bitcast.11, f32[4096,512]{1,0:T(8,128)S(1)} %bitcast.32), kind=kLoop, calls=%fused_computation.5 | loop fusion | flops 8388608 | bytes 41943044 | tf_op jit(solution)/shard_map/sub | solution.py:450
  (88 shorter events, 30.1 us)
Async XLA Ops:
  12.6 48.8 %collective-permute-start = (bf16[512,2048]{1,0:T(8,128)(2,1)}, bf16[512,2048]{1,0:T(8,128)(2,1)S(1)}, u32[]{:S(2)}, u32[]{:S(2)}) collective-permute-start(bf16[512,2048]{1,0:T(8,128)(2,1)} %pad_maximum_fusion.2), channel_id=1, source_target_pairs={{0,2},{2,0},{4,6},{6,4},{8,10},{10,8},{12,14},{14,12},{1,3},{3,1},... | collective-permute-start | bytes 6291464 | tf_op jit(solution)/shard_map/ppermute | solution.py:57
  15.6 46.4 %copy-start.3 = (bf16[512,4096]{1,0:T(8,128)(2,1)S(1)}, bf16[512,4096]{1,0:T(8,128)(2,1)}, u32[]{:S(2)}) copy-start(bf16[512,4096]{1,0:T(8,128)(2,1)} %copy-done.2) | copy-start | bytes 12582916
  64.1 24.4 %collective-permute-start.1 = (bf16[512,1024]{1,0:T(8,128)(2,1)S(1)}, bf16[512,1024]{1,0:T(8,128)(2,1)S(1)}, u32[]{:S(2)}, u32[]{:S(2)}) collective-permute-start(bf16[512,1024]{1,0:T(8,128)(2,1)S(1)} %pad_maximum_fusion.3), channel_id=1, source_target_pairs={{0,4},{2,6},{4,0},{6,2},{8,12},{10,14},{12,8},{14,10},{1,5},{3,7},... | collective-permute-start | bytes 3145736 | tf_op jit(solution)/shard_map/ppermute | solution.py:57
  93.4 24.4 %collective-permute-start.2 = (bf16[512,512]{1,0:T(8,128)(2,1)S(1)}, bf16[512,512]{1,0:T(8,128)(2,1)S(1)}, u32[]{:S(2)}, u32[]{:S(2)}) collective-permute-start(bf16[512,512]{1,0:T(8,128)(2,1)S(1)} %get-tuple-element.10), channel_id=1, source_target_pairs={{0,8},{2,10},{4,12},{6,14},{8,0},{10,2},{12,4},{14,6},{1,9},{3,11}... | collective-permute-start | bytes 1572872 | tf_op jit(solution)/shard_map/ppermute | solution.py:57
  119.1 2.0 collective-permute-start.3
  121.2 14.9 %collective-permute-start.4 = (bf16[256,512]{1,0:T(8,128)(2,1)S(1)}, bf16[256,512]{1,0:T(8,128)(2,1)S(1)}, u32[]{:S(2)}, u32[]{:S(2)}) collective-permute-start(bf16[256,512]{1,0:T(8,128)(2,1)S(1)} %constant_dynamic-slice_fusion), channel_id=1, source_target_pairs={{0,8},{2,10},{4,12},{6,14},{8,0},{10,2},{12,4},{14,6},{1,9},{3,11}... | collective-permute-start | bytes 786440 | tf_op jit(solution)/shard_map/ppermute | solution.py:71
  127.2 93.7 %collective-permute-start.9 = (bf16[4096,512]{1,0:T(8,128)(2,1)}, bf16[4096,512]{1,0:T(8,128)(2,1)}, u32[]{:S(2)}, u32[]{:S(2)}) collective-permute-start(bf16[4096,512]{1,0:T(8,128)(2,1)} %convert_element_type.84), channel_id=1, source_target_pairs={{0,1},{1,0},{2,3},{3,2},{4,5},{5,4},{6,7},{7,6},{8,9},{9,8},{10,11... | collective-permute-start | bytes 12582920 | tf_op jit(solution)/shard_map/ppermute | solution.py:24
  136.4 13.5 %collective-permute-start.5 = (bf16[256,1024]{1,0:T(8,128)(2,1)S(1)}, bf16[256,1024]{1,0:T(8,128)(2,1)S(1)}, u32[]{:S(2)}, u32[]{:S(2)}) collective-permute-start(bf16[256,1024]{1,0:T(8,128)(2,1)S(1)} %pad_maximum_fusion.6), channel_id=1, source_target_pairs={{0,4},{2,6},{4,0},{6,2},{8,12},{10,14},{12,8},{14,10},{1,5},{3,7},... | collective-permute-start | bytes 1572872 | tf_op jit(solution)/shard_map/ppermute | solution.py:71
  151.0 24.1 %collective-permute-start.6 = (bf16[256,2048]{1,0:T(8,128)(2,1)}, bf16[256,2048]{1,0:T(8,128)(2,1)S(1)}, u32[]{:S(2)}, u32[]{:S(2)}) collective-permute-start(bf16[256,2048]{1,0:T(8,128)(2,1)} %pad_maximum_fusion.4), channel_id=1, source_target_pairs={{0,2},{2,0},{4,6},{6,4},{8,10},{10,8},{12,14},{14,12},{1,3},{3,1},... | collective-permute-start | bytes 3145736 | tf_op jit(solution)/shard_map/ppermute | solution.py:71
  158.8 77.6 %collective-permute-start.8 = (bf16[2,512,512]{2,1,0:T(8,128)(2,1)}, bf16[2,512,512]{2,1,0:T(8,128)(2,1)}, u32[]{:S(2)}, u32[]{:S(2)}) collective-permute-start(bf16[2,512,512]{2,1,0:T(8,128)(2,1)} %pad_maximum_fusion.5), channel_id=1, source_target_pairs={{0,1},{17,16},{2,3},{19,18},{4,5},{21,20},{6,7},{23,22},{8,9},{25,... | collective-permute-start | bytes 3145736 | tf_op jit(solution)/shard_map/ppermute | solution.py:93
  181.7 54.9 %collective-permute-start.7 = (bf16[256,4096]{1,0:T(8,128)(2,1)}, bf16[256,4096]{1,0:T(8,128)(2,1)S(1)}, u32[]{:S(2)}, u32[]{:S(2)}) collective-permute-start(bf16[256,4096]{1,0:T(8,128)(2,1)} %select_dynamic-update-slice_fusion), channel_id=1, source_target_pairs={{0,16},{16,0},{1,17},{17,1},{2,18},{18,2},{3,19},{19,3},{4,20},{20... | collective-permute-start | bytes 6291464 | tf_op jit(solution)/shard_map/ppermute | solution.py:97
  236.6 9.7 %slice-start.4 = ((s8[8388608]{0:T(1024)(128)(4,1)}), s8[4194304]{0:T(1024)(128)(4,1)S(1)}, s32[]{:S(2)}) async-start(s8[8388608]{0:T(1024)(128)(4,1)} %bitcast.33), calls=%async_computation.4 | async-start | bytes 8388608
  238.6 7.7 copy-start.6
  238.7 7.6 copy-start.8
  238.7 7.6 slice-start.5
  244.7 14.1 %collective-permute-start.10 = (bf16[512,512]{1,0:T(8,128)(2,1)S(1)}, bf16[512,512]{1,0:T(8,128)(2,1)S(1)}, u32[]{:S(2)}, u32[]{:S(2)}) collective-permute-start(bf16[512,512]{1,0:T(8,128)(2,1)S(1)} %get-tuple-element.37), channel_id=1, source_target_pairs={{0,1},{1,0},{2,3},{3,2},{4,5},{5,4},{6,7},{7,6},{8,9},{9,8},{10,11... | collective-permute-start | bytes 1572872 | tf_op jit(solution)/shard_map/ppermute | solution.py:24
  246.3 12.5 %slice-start = ((s8[8388608]{0:T(1024)(128)(4,1)}), s8[4194304]{0:T(1024)(128)(4,1)S(1)}, s32[]{:S(2)}) async-start(s8[8388608]{0:T(1024)(128)(4,1)} %bitcast.29), calls=%async_computation | async-start | bytes 8388608
  251.2 7.6 slice-start.1
  258.8 12.5 %copy-start.5 = (f32[4096,512]{1,0:T(8,128)}, f32[4096,512]{1,0:T(8,128)S(1)}, u32[]{:S(2)}) copy-start(f32[4096,512]{1,0:T(8,128)S(1)} %multiply_add_fusion.1) | copy-start | bytes 25165828
  271.3 513.6 %copy-start.7 = (bf16[256,4096]{1,0:T(8,128)(2,1)S(1)}, bf16[256,4096]{1,0:T(8,128)(2,1)}, u32[]{:S(2)}) copy-start(bf16[256,4096]{1,0:T(8,128)(2,1)} %copy-done.6) | copy-start | bytes 6291460
  271.3 513.6 %copy-start.9 = (bf16[256,4096]{1,0:T(8,128)(2,1)S(1)}, bf16[256,4096]{1,0:T(8,128)(2,1)}, u32[]{:S(2)}) copy-start(bf16[256,4096]{1,0:T(8,128)(2,1)} %copy-done.8) | copy-start | bytes 6291460
  784.9 6.9 slice-start.6
  784.9 6.9 slice-start.7
  791.8 9.2 %collective-permute-start.11 = (bf16[512,512]{1,0:T(8,128)(2,1)S(1)}, bf16[512,512]{1,0:T(8,128)(2,1)S(1)}, u32[]{:S(2)}, u32[]{:S(2)}) collective-permute-start(bf16[512,512]{1,0:T(8,128)(2,1)S(1)} %get-tuple-element.39), channel_id=1, source_target_pairs={{0,1},{1,0},{2,3},{3,2},{4,5},{5,4},{6,7},{7,6},{8,9},{9,8},{10,11... | collective-permute-start | bytes 1572872 | tf_op jit(solution)/shard_map/ppermute | solution.py:24
  801.0 33.3 %slice-start.2 = ((s8[8388608]{0:T(1024)(128)(4,1)}), s8[4194304]{0:T(1024)(128)(4,1)S(1)}, s32[]{:S(2)}) async-start(s8[8388608]{0:T(1024)(128)(4,1)} %bitcast.31), calls=%async_computation.2 | async-start | bytes 8388608
  801.0 33.3 %slice-start.3 = ((s8[8388608]{0:T(1024)(128)(4,1)}), s8[4194304]{0:T(1024)(128)(4,1)S(1)}, s32[]{:S(2)}) async-start(s8[8388608]{0:T(1024)(128)(4,1)} %bitcast.31), calls=%async_computation.3 | async-start | bytes 8388608
  813.6 1.1 collective-permute-start.12
  816.0 3.5 collective-permute-start.13
  820.8 3.5 collective-permute-start.14
  824.4 3.5 collective-permute-start.15
  827.9 4.4 collective-permute-start.16
  834.3 11.2 %copy-start.1 = (bf16[1,512,1024]{2,1,0:T(8,128)(2,1)S(1)}, bf16[1,512,1024]{2,1,0:T(8,128)(2,1)}, u32[]{:S(2)}) copy-start(bf16[1,512,1024]{2,1,0:T(8,128)(2,1)} %param.6) | copy-start | bytes 3145732
  (3 other events, 5.9 us)

commit v3 on v2

--- a/solution.py
+++ b/solution.py
@@ -164,21 +164,27 @@
 
 UNITS = 16
 LATER = 48
+AHEAD = 2
 MESH = pl.DeviceIdType.MESH
 
 
 def gather_kernel(
-    g_ref, m_hbm, base_hbm, panel, res_hbm, app_hbm,
-    maps, rf, acc, prod, buf, col, base, own_sem, in_sem, col_sem, out_sem, zs, zr, ys, yr, bs, br, cs, cr, xs, xr,
+    ctx, g_ref, m_hbm, w_hbm, skip_hbm, cross_hbm, map_hbm,
+    panel, res_hbm, app_hbm, src_hbm, cols_hbm,
+    maps, rf, acc, prod, buf, col, base, old, part, ry, rz, pair, cols, states, ip_send, ip_recv, delta, inner,
+    own_sem, put_sem, in_sem, col_sem, out_sem, zs, zr, ys, yr, bs, br, cs, cr, xs, xr, mx, sy, sz, sc, sx, gz, gy, gc, ix,
 ):
     k, h, t = lax.axis_index("mp"), lax.axis_index("heads"), lax.axis_index("tok")
     z, y = h // 2, h % 2
-    height, width = g_ref.shape
+    height, width = g_ref.shape[0] * g_ref.shape[1], g_ref.shape[2]
     unit = height // UNITS
     early = unit - LATER
     chunks = rf.shape[0] // 2
+    per = UNITS // chunks
     step = height // chunks
     steps = ((1, 0), (-1, 1))
+    new_weight = (1.0 - decay_keep) / ctx.shape[0]
+    half_rows = pl.ds(pl.multiple_of(k * (step // 2), step // 2), step // 2)
 
     def block(zz, yy):
         return k * 8 + zz * 2 + yy
@@ -220,32 +226,92 @@
     def x_copy(tt, c):
         return remote(rf.at[tt * chunks + c], xs.at[c], xr.at[c], at_x)
 
-    own = pltpu.make_async_copy(g_ref, panel.at[block(z, y)], own_sem)
+    def send_maps(tt):
+        return remote(maps.at[pl.ds(tt * chunks, chunks)], mx.at[0], mx.at[1], at_x)
+
+    def part_y(yy):
+        return pltpu.make_async_remote_copy(
+            src_ref=part.at[yy], dst_ref=ry, send_sem=sy.at[0], recv_sem=sy.at[1],
+            device_id=at_y, device_id_type=MESH,
+        )
+
+    def line(zz):
+        return (k, zz * 2 + y, t)
+
+    def part_z(zz, to):
+        return pltpu.make_async_remote_copy(
+            src_ref=part.at[y, to], dst_ref=rz.at[zz], send_sem=sz.at[0, to], recv_sem=sz.at[1, zz],
+            device_id=line(to), device_id_type=MESH,
+        )
+
+    def pair_core(kk):
+        return remote(pair.at[kk], sc.at[0], sc.at[1], at_core)
+
+    def pair_x():
+        return pltpu.make_async_remote_copy(
+            src_ref=pair, dst_ref=cols, send_sem=sx.at[0], recv_sem=sx.at[1],
+            device_id=at_x, device_id_type=MESH,
+        )
+
+    def source_z(zz, to):
+        return remote(states.at[y, zz, half_rows], gz.at[0, to], gz.at[1, zz], line(to))
+
+    def source_y(yy):
+        return remote(states.at[yy, :, half_rows], gy.at[0], gy.at[1], at_y)
+
+    def source_core(kk):
+        rows = pl.ds(pl.multiple_of(kk * (step // 2), step // 2), step // 2)
+        return remote(states.at[:, :, rows], gc.at[0], gc.at[1], at_core)
+
+    def inner_x(n):
+        return pltpu.make_async_remote_copy(
+            src_ref=ip_send.at[n], dst_ref=ip_recv.at[n], send_sem=ix.at[0, n], recv_sem=ix.at[1, n],
+            device_id=at_x, device_id_type=MESH,
+        )
+
+    def feature(c):
+        return states[c % 2, c // 2]
+
+    def low_rank(c):
+        return lax.dot_general(feature(c), delta[...], (((0,), (0,)), ((), ())), preferred_element_type=f32)
+
+    own = pltpu.make_async_copy(g_ref, buf.at[pl.ds(0, chunks)], own_sem)
     own.start()
-    load_maps = pltpu.make_async_copy(m_hbm, maps, in_sem)
+    load_maps = pltpu.make_async_copy(m_hbm, maps.at[pl.ds(t * chunks, chunks)], in_sem)
     load_maps.start()
     barrier = pltpu.get_barrier_semaphore()
     for dev in (at_y, at_core, at_x):
         pl.semaphore_signal(barrier, inc=1, device_id=dev, device_id_type=MESH)
-    for dz, d in steps:
-        @pl.when(inside(z + dz))
-        def _():
-            pl.semaphore_signal(barrier, inc=1, device_id=at_z(dz), device_id_type=MESH)
-    pl.semaphore_wait(barrier, 3 + jnp.where(z > 0, 1, 0) + jnp.where(z < 3, 1, 0))
+    for dz in range(1, 4):
+        pl.semaphore_signal(barrier, inc=1, device_id=line((z + dz) % 4), device_id_type=MESH)
     own.wait()
+
+    def put(c):
+        return pltpu.make_async_copy(
+            buf.at[c], panel.at[block(z, y), pl.ds(c * step, step)], put_sem.at[c]
+        )
+
+    for c in range(8):
+        put(c).start()
     load_maps.wait()
+    pl.semaphore_wait(barrier, 6)
+    for c in range(8):
+        put(c).wait()
+    send_maps(t).start()
 
     def valid(u):
         return (u >= 0) & (u < UNITS)
 
     def product_one(c):
-        for half in range(2):
-            core_copy(1 - k, 2 * c + half).wait_recv()
+        for part in range(per):
+            core_copy(1 - k, per * c + part).wait_recv()
         rows = pl.ds(pl.multiple_of(c * step, step), step)
         load = pltpu.make_async_copy(panel.at[:, rows], buf, in_sem)
         load.start()
-        load_base = pltpu.make_async_copy(base_hbm.at[rows], base, own_sem)
+        load_base = pltpu.make_async_copy(cross_hbm.at[rows], base, own_sem)
         load_base.start()
+        load_old = pltpu.make_async_copy(map_hbm.at[rows], old, col_sem.at[0, 0])
+        load_old.start()
         load.wait()
         prod[...] = jnp.zeros_like(prod)
 
@@ -256,7 +322,8 @@
             )
 
         load_base.wait()
-        base[...] = base[...] - decay_keep * prod[...]
+        load_old.wait()
+        base[...] = decay_keep * (base[...] - prod[...]) - ridge_weight * old[...] + new_weight * low_rank(c)
         rf[t * chunks + c] = base[...].astype(bf16)
         x_copy(t, c).start()
         save = pltpu.make_async_copy(base, res_hbm.at[rows], out_sem)
@@ -270,7 +337,21 @@
             )
 
         acc[c] = prod[...]
+        prod[...] = jnp.dot(feature(c), rf[t * chunks + c], preferred_element_type=f32)
         save.wait()
+
+        @pl.when(c == 0)
+        def _():
+            inner[...] = prod[...]
+
+        @pl.when(c > 0)
+        def _():
+            inner[...] += prod[...]
+
+        @pl.when(c == chunks - 1)
+        def _():
+            ip_send[1] = inner[...].astype(bf16)
+            inner_x(1).start()
 
     def column(c, i, slot, o):
         return pltpu.make_async_copy(
@@ -299,7 +380,7 @@
                 col[slot, 1], rf[chunks + c], preferred_element_type=f32
             )
 
-    @pl.loop(0, UNITS + 6)
+    @pl.loop(0, UNITS + 4 * AHEAD + per // 2 + 2)
     def _(tick):
         u0 = tick
 
@@ -312,7 +393,7 @@
             y_copy(z, y, u0, unit).start()
 
         for lag in range(1, 5):
-            u = tick - lag
+            u = tick - lag * AHEAD
 
             @pl.when(valid(u))
             def _():
@@ -349,18 +430,137 @@
                 if lag == 4:
                     core_copy(k, u).start()
 
-        w = tick - 6
-
-        @pl.when((w >= 0) & (w % 2 == 0))
-        def _():
-            product_one(w // 2)
-
-        @pl.when((w >= 0) & (w % 2 == 1))
-        def _():
-            product_two(w // 2)
+        @pl.when(tick == 0)
+        def _():
+            def weights(i, slot, o):
+                return pltpu.make_async_copy(
+                    w_hbm.at[pl.ds(o * step, step), pl.ds(pl.multiple_of(i * step, step), step)],
+                    col.at[slot, o],
+                    col_sem.at[slot, o],
+                )
+
+            for o in range(2):
+                weights(0, 0, o).start()
+
+            @pl.loop(0, 8)
+            def _(i):
+                slot = i % 2
+
+                @pl.when(i < 7)
+                def _():
+                    for o in range(2):
+                        weights(i + 1, 1 - slot, o).start()
+
+                for o in range(2):
+                    weights(i, slot, o).wait()
+                part[i % 2, i // 2] = (
+                    jnp.dot(ctx[:, :step], col[slot, 0], preferred_element_type=f32)
+                    + jnp.dot(ctx[:, step:], col[slot, 1], preferred_element_type=f32)
+                ).astype(bf16)
+
+            part_y(1 - y).start()
+
+        @pl.when(tick == 4)
+        def _():
+            part_y(1 - y).wait_send()
+            part_y(1 - y).wait_recv()
+
+            @pl.loop(0, 4)
+            def _(i):
+                part[y, i] = (part[y, i].astype(f32) + ry[i].astype(f32)).astype(bf16)
+
+            for dz in range(1, 4):
+                part_z(z, (z + dz) % 4).start()
+
+        @pl.when(tick == 6)
+        def _():
+            load = pltpu.make_async_copy(
+                skip_hbm.at[k, :, pl.ds(pl.multiple_of(h * step, step), step)], delta, own_sem
+            )
+            load.start()
+            total = part[y, z].astype(f32)
+            for dz in range(1, 4):
+                part_z((z + dz) % 4, z).wait_recv()
+                total = total + rz[(z + dz) % 4].astype(f32)
+            load.wait()
+            pair[k] = (total + delta[...].astype(f32)).astype(bf16)
+            pair_core(k).start()
+            pair_core(1 - k).wait_recv()
+            states[y, z, half_rows] = pair[0, half_rows]
+            for dz in range(1, 4):
+                source_z(z, (z + dz) % 4).start()
+
+            @pl.when(k == t)
+            def _():
+                pair_x().start()
+                cols[...] = pair[...]
+
+        @pl.when(tick == 8)
+        def _():
+            for dz in range(1, 4):
+                source_z((z + dz) % 4, z).wait_recv()
+            source_y(y).start()
+
+        @pl.when(tick == 9)
+        def _():
+            source_y(1 - y).wait_recv()
+            source_core(k).start()
+            source_core(1 - k).wait_recv()
+            prod[...] = jnp.zeros_like(prod)
+
+            @pl.loop(0, chunks)
+            def _(c):
+                prod[...] += jnp.dot(feature(c), maps[t * chunks + c], preferred_element_type=f32)
+
+            ip_send[0] = prod[...].astype(bf16)
+            inner_x(0).start()
+
+        @pl.when(tick == 11)
+        def _():
+            @pl.when(k != t)
+            def _():
+                pair_x().wait_recv()
+
+            inner_x(0).wait_recv()
+            delta[...] = (cols[1].astype(f32) - prod[...] - ip_recv[0].astype(f32)).astype(bf16)
+            send_maps(1 - t).wait_recv()
+
+        w = tick - 4 * AHEAD - per - 1
+
+        @pl.when((w >= 0) & (w % per == 0))
+        def _():
+            product_one(w // per)
+
+        @pl.when((w >= 0) & (w % per == per // 2))
+        def _():
+            product_two(w // per)
+
+    inner_x(1).wait_recv()
+    delta[...] = (inner[...] + ip_recv[1].astype(f32)).astype(bf16)
+
+    @pl.loop(0, chunks)
+    def _(c):
+        acc[c] = decay_keep * acc[c] + new_weight * low_rank(c)
 
     save = pltpu.make_async_copy(acc, app_hbm, out_sem)
     save.start()
+    save_source = pltpu.make_async_copy(states, src_hbm, own_sem)
+    save_source.start()
+    save_cols = pltpu.make_async_copy(cols, cols_hbm, in_sem)
+    save_cols.start()
+    send_maps(t).wait_send()
+    for dz in range(1, 4):
+        part_z(z, (z + dz) % 4).wait_send()
+        source_z(z, (z + dz) % 4).wait_send()
+    pair_core(k).wait_send()
+    source_y(y).wait_send()
+    source_core(k).wait_send()
+    for n in range(2):
+        inner_x(n).wait_send()
+
+    @pl.when(k == t)
+    def _():
+        pair_x().wait_send()
 
     @pl.loop(0, UNITS)
     def _(u):
@@ -383,66 +583,76 @@
         x_copy(t, c).wait_send()
 
     save.wait()
-
-
-def gather_and_multiply(gram_half, maps, base):
+    save_source.wait()
+    save_cols.wait()
+
+
+def gather_and_multiply(context, gram_half, map_half, out_weight, skip_states, cross_old, map_old):
     height, width = gram_half.shape
     chunks = 8
     step = height // chunks
     any_space = pl.BlockSpec(memory_space=pltpu.HBM)
     dma = pltpu.SemaphoreType.DMA
-    panel, residual, applied = pl.pallas_call(
+    tile = (step, width)
+    _, residual, product, source, cols = pl.pallas_call(
         gather_kernel,
         out_shape=[
             jax.ShapeDtypeStruct((16, height, width), bf16),
             jax.ShapeDtypeStruct((height, width), f32),
-            jax.ShapeDtypeStruct((chunks, step, width), f32),
+            jax.ShapeDtypeStruct((chunks, *tile), f32),
+            jax.ShapeDtypeStruct((2, 4, *tile), bf16),
+            jax.ShapeDtypeStruct((2, *tile), bf16),
         ],
-        in_specs=[any_space] * 3,
-        out_specs=[any_space] * 3,
+        in_specs=[pl.BlockSpec(memory_space=pltpu.VMEM)] + [any_space] * 6,
+        out_specs=[any_space] * 5,
         scratch_shapes=[
-            pltpu.VMEM((16, step, width), bf16),
-            pltpu.VMEM((16, step, width), bf16),
-            pltpu.VMEM((chunks, step, width), f32),
-            pltpu.VMEM((step, width), f32),
-            pltpu.VMEM((16, step, width), bf16),
-            pltpu.VMEM((2, 2, step, width), bf16),
-            pltpu.VMEM((step, width), f32),
-            dma, dma, dma((2, 2)), dma,
+            pltpu.VMEM((16, *tile), bf16),
+            pltpu.VMEM((16, *tile), bf16),
+            pltpu.VMEM((chunks, *tile), f32),
+            pltpu.VMEM(tile, f32),
+            pltpu.VMEM((16, *tile), bf16),
+            pltpu.VMEM((2, 2, *tile), bf16),
+            pltpu.VMEM(tile, f32),
+            pltpu.VMEM(tile, f32),
+            pltpu.VMEM((2, 4, *tile), bf16),
+            pltpu.VMEM((4, *tile), bf16),
+            pltpu.VMEM((4, *tile), bf16),
+            pltpu.VMEM((2, *tile), bf16),
+            pltpu.VMEM((2, *tile), bf16),
+            pltpu.VMEM((2, 4, *tile), bf16),
+            pltpu.VMEM((2, *tile), bf16),
+            pltpu.VMEM((2, *tile), bf16),
+            pltpu.VMEM(tile, bf16),
+            pltpu.VMEM(tile, f32),
+            dma, dma((chunks,)), dma, dma((2, 2)), dma,
             dma((2, 3, UNITS)), dma((2, 3, UNITS)),
             dma((4, UNITS)), dma((4, UNITS)),
             dma((2, 3, UNITS)), dma((2, 3, UNITS)),
             dma((UNITS,)), dma((UNITS,)),
             dma((chunks,)), dma((chunks,)),
+            dma((2,)), dma((2,)), dma((2, 4)), dma((2,)), dma((2,)), dma((2, 4)), dma((2,)), dma((2,)), dma((2, 2)),
         ],
         compiler_params=pltpu.CompilerParams(
-            collective_id=0, has_side_effects=True, vmem_limit_bytes=56 * 1024 * 1024
+            collective_id=0, has_side_effects=True, vmem_limit_bytes=60 * 1024 * 1024
         ),
-        cost_estimate=pl.CostEstimate(
-            flops=4 * height * width * 16 * width, bytes_accessed=16 * height * width * 6, transcendentals=0
-        ),
-    )(gram_half, maps.reshape(16, step, width), base)
-    return residual, applied.reshape(height, width)
+    )(
+        context, gram_half.reshape(chunks, *tile), map_half.reshape(chunks, *tile),
+        out_weight, skip_states, cross_old, map_old,
+    )
+    return residual, product.reshape(height, width), source, cols
 
 
 def with_kernel(context, out_weight, skip_states, gram_old, cross_old, map_old):
-    t = lax.axis_index("tok")
     tokens = context.shape[1]
-    width = gram_old.shape[1]
+    height, width = gram_old.shape
     new_weight = (1.0 - decay_keep) / tokens
-    map_half = map_old.astype(bf16)
-    map_away = shifted(map_half, "tok", 1)
-    maps = jnp.concatenate(
-        [jnp.where(t == 0, map_half, map_away), jnp.where(t == 0, map_away, map_half)], 0
+    residual, product, source, cols = gather_and_multiply(
+        context[0], gram_old.astype(bf16), map_old.astype(bf16), out_weight[0], skip_states, cross_old, map_old
     )
-    source, source_cols, target_cols = make_states(context, out_weight, skip_states, width)
-    inner_map = sum_tok(dot(source, map_half))
-    cross_new = decay_keep * cross_old + new_weight * token_inner(source, target_cols)
-    base = cross_new - new_weight * token_inner(source, inner_map) - ridge_weight * map_old
-    residual, product = gather_and_multiply(gram_old.astype(bf16), maps, base)
-    gram_new = decay_keep * gram_old + new_weight * token_inner(source, source_cols)
-    inner_residual = sum_tok(dot(source, residual.astype(bf16)))
-    applied = decay_keep * product + new_weight * token_inner(source, inner_residual) + ridge_weight * residual
+    source = jnp.concatenate([source[i % 2, i // 2] for i in range(8)], 1)
+    gram_new = decay_keep * gram_old + new_weight * token_inner(source, cols[0])
+    cross_new = decay_keep * cross_old + new_weight * token_inner(source, cols[1])
+    applied = product + ridge_weight * residual
     totals = jnp.stack([jnp.sum(residual * residual), jnp.sum(residual * applied)])
     for axis in ("mp", "tok", "heads"):
         totals = total_over(totals, axis)

time: 847 us -> 571 us (0.67)
  waiting for transfers between devices: 184 us -> 11.4 us
  matrix products: 57.2 us -> 12.5 us
  other arithmetic: 68.1 us -> 32.5 us
  starting transfers between devices: 17.1 us -> 3.73 us
    ppermute x12 -> x0, waiting for transfers between devices: 169 us -> none  [the longest x3 90.2 us: scatter_sum(): got = lax.ppermute(send, axis, [(i, i ^ bit) for i in range(n)]).astype(f32)]
    dot_general x4 -> x2, matrix products: 36.2 us -> 12.5 us  [token_inner(): lax.dot_general(left, right, (((0,), (0,)), ((), ())), preferred_element_...]
    dot_general x3 -> x0, matrix products: 21 us -> none  [dot(): return jnp.dot(a, b, preferred_element_type=f32)]
    ppermute x12 -> x0, starting transfers between devices: 15.4 us -> none  [the longest x3 7.39 us: scatter_sum(): got = lax.ppermute(send, axis, [(i, i ^ bit) for i in range(n)]).astype(f32)]
    concatenate x6 -> x0, other arithmetic: 11.5 us -> none  [the longest x1 7.4 us: with_kernel(): jnp.concatenate([jnp.where(t == 0, map_half, map_away), jnp.where(t == 0,...]
    select_n x7 -> x0, other arithmetic: 10.7 us -> none  [the longest x1 8.07 us: with_kernel(): jnp.where(t == 0, map_half, map_away)]
    convert_element_type x7 -> x2, other arithmetic: 19.5 us -> 8.8 us  [the longest x1 6.24 us: with_kernel(): gram_old.astype(bf16)]
  transfers between devices with their start and end apart: 17 -> 5, of which waited for: 14 -> 4; matrix products, arithmetic and copies ran while one was open for 6% -> 2% of each run, Pallas kernels for 0% -> 0%
where the time goes in v3:
time: 571 us; the launch traced here: 570 us
  Pallas kernels  506 us (89%)
  other arithmetic  32.5 us (6%)
  matrix products  12.5 us (2%)
  waiting for transfers between devices  11.4 us (2%)
    pallas_call x1, Pallas kernels, gather_and_multiply(): pl.pallas_call(gather_kernel, out_shape=[jax.ShapeDtypeStruct((16, height...  506 us
    dot_general x2, matrix products, token_inner(): lax.dot_general(left, right, (((0,), (0,)), ((), ())), preferred_element_...  12.5 us
  transfers between devices with their start and end apart: 5, of which 4 were waited for; matrix products, arithmetic and copies ran while one was open for 2% of the time, Pallas kernels for 0%

profile of v3, /device:TPU:0, one launch (start us, length us, event | category | flops | bytes accessed | tf_op | source)
XLA Modules:
  0.0 570.4 jit_solution(2761289476656636969)
XLA Ops:
  0.6 6.2 %convert_element_type.6 = bf16[4096,512]{1,0:T(8,128)(2,1)} convert(f32[4096,512]{1,0:T(8,128)} %param.9) | non-fusion elementwise | flops 2097152 | bytes 12582912 | tf_op jit(solution)/shard_map/convert_element_type | solution.py:650
  6.9 1.0 copy-done
  7.9 2.6 convert_element_type.7
  10.5 505.8 %shard_map.93 = (bf16[16,4096,512]{2,1,0:T(8,128)(2,1)}, f32[4096,512]{1,0:T(8,128)}, f32[8,512,512]{2,1,0:T(8,128)}, bf16[2,4,512,512]{3,2,1,0:T(8,128)(2,1)}, bf16[2,512,512]{2,1,0:T(8,128)(2,1)}) custom-call(bf16[512,1024]{1,0:T(8,128)(2,1)} %bitcast.46, bf16[8,512,512]{2,1,0:T(8,128)(2,1)} %bitcast.43, bf16[8,512,512]{2,1,0:T(8,128)(2,1)} %bitcast.44, ...), custom_call_target="tpu_custom_call" | custom-call | tf_op jit(solution)/shard_map/pallas_call | solution.py:597
  516.3 0.0 slice-start.4
  516.3 7.9 %multiply_reduce_fusion.1 = (f32[]{:T(128)}, f32[]{:T(128)}) fusion(f32[4096,512]{1,0:T(8,128)} %get-tuple-element.10, f32[8,512,512]{2,1,0:T(8,128)} %get-tuple-element.11), kind=kLoop, calls=%fused_computation.4 | loop fusion | flops 12582910 | bytes 16777224 | tf_op jit(solution)/shard_map/reduce_sum | solution.py:656
  524.3 2.0 pad_maximum_fusion
  526.2 0.0 collective-permute-start
  526.3 0.1 bitcast_dynamic-update-slice_fusion.7
  526.3 0.1 bitcast_dynamic-update-slice_fusion.6
  526.4 0.1 bitcast_dynamic-update-slice_fusion.5
  526.5 0.1 bitcast_dynamic-update-slice_fusion.4
  526.6 0.1 bitcast_dynamic-update-slice_fusion.3
  526.6 0.1 bitcast_dynamic-update-slice_fusion.2
  526.7 0.0 slice-start.2
  526.7 0.1 bitcast_dynamic-update-slice_fusion.1
  526.8 0.1 bitcast_dynamic-update-slice_fusion
  526.9 0.0 slice-start.3
  527.0 6.3 %multiply_add_fusion.1 = f32[4096,512]{1,0:T(8,128)} fusion(f32[4096,512]{1,0:T(8,128)S(1)} %bitcast.42, bf16[512,4096]{1,0:T(8,128)(2,1)S(1)} %bitcast_dynamic-update-slice_fusion, bf16[2,512,512]{2,1,0:T(8,128)(2,1)S(1)} %copy-done.2), kind=kOutput, calls=%fused_computation.5 | convolution fusion | flops 2153775104 | bytes 21495808 | tf_op jit(solution)/shard_map/dot_general | solution.py:19
  533.3 6.2 %multiply_add_fusion.2 = f32[4096,512]{1,0:T(8,128)} fusion(f32[4096,512]{1,0:T(8,128)S(1)} %bitcast.40, bf16[512,4096]{1,0:T(8,128)(2,1)S(1)} %bitcast_dynamic-update-slice_fusion, bf16[2,512,512]{2,1,0:T(8,128)(2,1)S(1)} %copy-done.2), kind=kOutput, calls=%fused_computation.6 | convolution fusion | flops 2153775104 | bytes 21495808 | tf_op jit(solution)/shard_map/dot_general | solution.py:19
  539.5 1.4 fusion.7
  540.9 1.5 collective-permute-start.1
  542.4 2.0 collective-permute-done.1
  544.4 1.4 fusion.8
  545.8 0.5 collective-permute-start.2
  546.3 3.0 collective-permute-done.2
  549.3 0.3 collective-permute-start.3
  549.7 3.2 collective-permute-done.3
  552.9 1.4 collective-permute-start.4
  554.2 3.1 collective-permute-done.4
  557.3 0.6 fusion.4
  559.3 11.1 %multiply_subtract_fusion = (f32[4096,512]{1,0:T(8,128)}, f32[4096,512]{1,0:T(8,128)}) fusion(f32[4096,512]{1,0:T(8,128)} %get-tuple-element.10, f32[8,512,512]{2,1,0:T(8,128)} %get-tuple-element.11, f32[]{:T(128)} %bitcast.17, f32[4096,512]{1,0:T(8,128)S(1)} %bitcast.38), kind=kLoop, calls=%fused_computation.1 | loop fusion | flops 12582912 | bytes 41943044 | tf_op jit(solution)/shard_map/sub | solution.py:660
  (21 shorter events, 0.0 us)
Async XLA Ops:
  0.6 7.3 %copy-start = (f32[4096,512]{1,0:T(8,128)S(1)}, f32[4096,512]{1,0:T(8,128)}, u32[]{:S(2)}) copy-start(f32[4096,512]{1,0:T(8,128)} %map_hbm.1) | copy-start | bytes 25165828
  516.3 10.6 %slice-start.4 = ((s8[8388608]{0:T(1024)(128)(4,1)}), s8[4194304]{0:T(1024)(128)(4,1)S(1)}, s32[]{:S(2)}) async-start(s8[8388608]{0:T(1024)(128)(4,1)} %bitcast.41), calls=%async_computation.4 | async-start | bytes 8388608
  516.3 9.9 %copy-start.1 = (bf16[2,4,512,512]{3,2,1,0:T(8,128)(2,1)S(1)}, bf16[2,4,512,512]{3,2,1,0:T(8,128)(2,1)}, u32[]{:S(2)}) copy-start(bf16[2,4,512,512]{3,2,1,0:T(8,128)(2,1)} %get-tuple-element.8) | copy-start | bytes 12582916
  516.3 10.6 %slice-start.5 = ((s8[8388608]{0:T(1024)(128)(4,1)}), s8[4194304]{0:T(1024)(128)(4,1)S(1)}, s32[]{:S(2)}) async-start(s8[8388608]{0:T(1024)(128)(4,1)} %bitcast.41), calls=%async_computation.5 | async-start | bytes 8388608
  524.3 2.6 copy-start.2
  526.2 13.3 %collective-permute-start = (f32[2]{0:T(128)S(1)}, f32[2]{0:T(128)S(1)}, u32[]{:S(2)}, u32[]{:S(2)}) collective-permute-start(f32[2]{0:T(128)S(1)} %pad_maximum_fusion), channel_id=1, source_target_pairs={{0,16},{16,0},{1,17},{17,1},{2,18},{18,2},{3,19},{19,3},{4,20},{20... | collective-permute-start | bytes 32 | tf_op jit(solution)/shard_map/ppermute | solution.py:33
  526.7 6.6 %slice-start.2 = ((s8[8388608]{0:T(1024)(128)(4,1)}), s8[4194304]{0:T(1024)(128)(4,1)S(1)}, s32[]{:S(2)}) async-start(s8[8388608]{0:T(1024)(128)(4,1)} %bitcast.39), calls=%async_computation.2 | async-start | bytes 8388608
  526.9 6.4 %slice-start.3 = ((s8[8388608]{0:T(1024)(128)(4,1)}), s8[4194304]{0:T(1024)(128)(4,1)S(1)}, s32[]{:S(2)}) async-start(s8[8388608]{0:T(1024)(128)(4,1)} %bitcast.39), calls=%async_computation.3 | async-start | bytes 8388608
  526.9 32.3 %slice-start = ((s8[8388608]{0:T(1024)(128)(4,1)}), s8[4194304]{0:T(1024)(128)(4,1)S(1)}, s32[]{:S(2)}) async-start(s8[8388608]{0:T(1024)(128)(4,1)} %bitcast.37), calls=%async_computation | async-start | bytes 8388608
  533.3 26.0 %slice-start.1 = ((s8[8388608]{0:T(1024)(128)(4,1)}), s8[4194304]{0:T(1024)(128)(4,1)S(1)}, s32[]{:S(2)}) async-start(s8[8388608]{0:T(1024)(128)(4,1)} %bitcast.37), calls=%async_computation.1 | async-start | bytes 8388608
  540.9 3.5 collective-permute-start.1
  545.8 3.5 collective-permute-start.2
  549.3 3.5 collective-permute-start.3
  552.9 4.4 collective-permute-start.4

commit v4 on v3

--- a/solution.py
+++ b/solution.py
@@ -164,7 +164,9 @@
 
 UNITS = 16
 LATER = 48
-AHEAD = 2
+AHEAD = 1
+EARLY = 1
+PHASES = (3, 5, 6, 7, 9)
 MESH = pl.DeviceIdType.MESH
 
 
@@ -207,6 +209,20 @@
     at_core = (1 - k, h, t)
     at_x = (k, h, 1 - t)
 
+    def own_copy(u, send, recv, dev):
+        return pltpu.make_async_remote_copy(
+            src_ref=g_ref.at[u // per, pl.ds(pl.multiple_of((u % per) * unit, unit), unit)],
+            dst_ref=piece(z, y, u, 0, unit),
+            send_sem=send, recv_sem=recv, device_id=dev, device_id_type=MESH,
+        )
+
+    def send_own(u):
+        for dz, d in steps:
+            @pl.when(inside(z + dz))
+            def _():
+                own_copy(u, zs.at[d, 0, u], zr.at[d, 0, u], at_z(dz)).start()
+        own_copy(u, ys.at[z, u], yr.at[z, u], at_y).start()
+
     def z_copy(s, dz, d, zz, u):
         return remote(piece(jnp.clip(zz, 0, 3), y, u, 0, unit), zs.at[d, s, u], zr.at[d, s, u], at_z(dz))
 
@@ -284,20 +300,15 @@
         pl.semaphore_signal(barrier, inc=1, device_id=dev, device_id_type=MESH)
     for dz in range(1, 4):
         pl.semaphore_signal(barrier, inc=1, device_id=line((z + dz) % 4), device_id_type=MESH)
-    own.wait()
 
     def put(c):
         return pltpu.make_async_copy(
             buf.at[c], panel.at[block(z, y), pl.ds(c * step, step)], put_sem.at[c]
         )
 
-    for c in range(8):
-        put(c).start()
-    load_maps.wait()
     pl.semaphore_wait(barrier, 6)
-    for c in range(8):
-        put(c).wait()
-    send_maps(t).start()
+    for u in range(EARLY):
+        send_own(u)
 
     def valid(u):
         return (u >= 0) & (u < UNITS)
@@ -315,10 +326,10 @@
         load.wait()
         prod[...] = jnp.zeros_like(prod)
 
-        @pl.loop(0, 8)
+        @pl.loop(0, 4)
         def _(q):
-            prod[...] += jnp.dot(buf[2 * q], maps[2 * q], preferred_element_type=f32) + jnp.dot(
-                buf[2 * q + 1], maps[2 * q + 1], preferred_element_type=f32
+            prod[...] += sum(
+                jnp.dot(buf[4 * q + i], maps[4 * q + i], preferred_element_type=f32) for i in range(4)
             )
 
         load_base.wait()
@@ -380,17 +391,11 @@
                 col[slot, 1], rf[chunks + c], preferred_element_type=f32
             )
 
-    @pl.loop(0, UNITS + 4 * AHEAD + per // 2 + 2)
+    @pl.loop(0, UNITS + 4 * AHEAD + per)
     def _(tick):
-        u0 = tick
-
-        @pl.when(u0 < UNITS)
-        def _():
-            for dz, d in steps:
-                @pl.when(inside(z + dz))
-                def _():
-                    z_copy(0, dz, d, z, u0).start()
-            y_copy(z, y, u0, unit).start()
+        @pl.when(tick + EARLY < UNITS)
+        def _():
+            send_own(tick + EARLY)
 
         for lag in range(1, 5):
             u = tick - lag * AHEAD
@@ -441,6 +446,11 @@
 
             for o in range(2):
                 weights(0, 0, o).start()
+            own.wait()
+            for c in range(8):
+                put(c).start()
+            load_maps.wait()
+            send_maps(t).start()
 
             @pl.loop(0, 8)
             def _(i):
@@ -459,8 +469,10 @@
                 ).astype(bf16)
 
             part_y(1 - y).start()
-
-        @pl.when(tick == 4)
+            for c in range(8):
+                put(c).wait()
+
+        @pl.when(tick == PHASES[0])
         def _():
             part_y(1 - y).wait_send()
             part_y(1 - y).wait_recv()
@@ -472,7 +484,7 @@
             for dz in range(1, 4):
                 part_z(z, (z + dz) % 4).start()
 
-        @pl.when(tick == 6)
+        @pl.when(tick == PHASES[1])
         def _():
             load = pltpu.make_async_copy(
                 skip_hbm.at[k, :, pl.ds(pl.multiple_of(h * step, step), step)], delta, own_sem
@@ -495,13 +507,13 @@
                 pair_x().start()
                 cols[...] = pair[...]
 
-        @pl.when(tick == 8)
+        @pl.when(tick == PHASES[2])
         def _():
             for dz in range(1, 4):
                 source_z((z + dz) % 4, z).wait_recv()
             source_y(y).start()
 
-        @pl.when(tick == 9)
+        @pl.when(tick == PHASES[3])
         def _():
             source_y(1 - y).wait_recv()
             source_core(k).start()
@@ -515,7 +527,7 @@
             ip_send[0] = prod[...].astype(bf16)
             inner_x(0).start()
 
-        @pl.when(tick == 11)
+        @pl.when(tick == PHASES[4])
         def _():
             @pl.when(k != t)
             def _():
@@ -525,15 +537,24 @@
             delta[...] = (cols[1].astype(f32) - prod[...] - ip_recv[0].astype(f32)).astype(bf16)
             send_maps(1 - t).wait_recv()
 
-        w = tick - 4 * AHEAD - per - 1
-
-        @pl.when((w >= 0) & (w % per == 0))
-        def _():
-            product_one(w // per)
-
-        @pl.when((w >= 0) & (w % per == per // 2))
-        def _():
-            product_two(w // per)
+        first = PHASES[-1]
+        behind = 2 * first - 6
+
+        def chunk_of(at):
+            busy = (at >= first) & ((at <= behind) | (at % 2 == 0)) & (at < 2 * chunks + 6)
+            return busy, jnp.where(at <= behind, at - first, (at - 6) // 2)
+
+        busy_two, chunk_two = chunk_of(tick - 1)
+
+        @pl.when(busy_two)
+        def _():
+            product_two(chunk_two)
+
+        busy_one, chunk_one = chunk_of(tick)
+
+        @pl.when(busy_one)
+        def _():
+            product_one(chunk_one)
 
     inner_x(1).wait_recv()
     delta[...] = (inner[...] + ip_recv[1].astype(f32)).astype(bf16)
@@ -650,12 +671,15 @@
         context[0], gram_old.astype(bf16), map_old.astype(bf16), out_weight[0], skip_states, cross_old, map_old
     )
     source = jnp.concatenate([source[i % 2, i // 2] for i in range(8)], 1)
-    gram_new = decay_keep * gram_old + new_weight * token_inner(source, cols[0])
-    cross_new = decay_keep * cross_old + new_weight * token_inner(source, cols[1])
     applied = product + ridge_weight * residual
     totals = jnp.stack([jnp.sum(residual * residual), jnp.sum(residual * applied)])
-    for axis in ("mp", "tok", "heads"):
-        totals = total_over(totals, axis)
+    totals = total_over(totals, "mp")
+    totals, source_cols = lax.optimization_barrier((totals, cols[0]))
+    gram_new = decay_keep * gram_old + new_weight * token_inner(source, source_cols)
+    totals = total_over(totals, "tok")
+    totals, target_cols = lax.optimization_barrier((totals, cols[1]))
+    cross_new = decay_keep * cross_old + new_weight * token_inner(source, target_cols)
+    totals = total_over(totals, "heads")
     step_size = totals[0] / totals[1]
     return gram_new, cross_new, map_old + step_size * residual, residual - step_size * applied
 

time: 571 us -> 541 us (0.947)
  Pallas kernels: 506 us -> 481 us
    pallas_call x1, Pallas kernels: 506 us -> 481 us  [gather_and_multiply(): pl.pallas_call(gather_kernel, out_shape=[jax.ShapeDtypeStruct((16, height...]
  transfers between devices with their start and end apart: 5 -> 5, of which waited for: 4 -> 3; matrix products, arithmetic and copies ran while one was open for 2% -> 2% of each run, Pallas kernels for 0% -> 0%
where the time goes in v4:
time: 541 us; the launch traced here: 540 us
  Pallas kernels  481 us (89%)
  other arithmetic  31.3 us (6%)
  matrix products  12.4 us (2%)
  waiting for transfers between devices  8.37 us (2%)
    pallas_call x1, Pallas kernels, gather_and_multiply(): pl.pallas_call(gather_kernel, out_shape=[jax.ShapeDtypeStruct((16, height...  481 us
    dot_general x2, matrix products, token_inner(): lax.dot_general(left, right, (((0,), (0,)), ((), ())), preferred_element_...  12.4 us
    sub x1, other arithmetic, with_kernel(): residual - step_size * applied  11.1 us
  transfers between devices with their start and end apart: 5, of which 3 were waited for; matrix products, arithmetic and copies ran while one was open for 2% of the time, Pallas kernels for 0%

profile of v4, /device:TPU:0, one launch (start us, length us, event | category | flops | bytes accessed | tf_op | source)
XLA Modules:
  0.0 540.1 jit_solution(2537491508019202380)
XLA Ops:
  0.6 0.0 copy-start
  0.6 6.2 %convert_element_type.6 = bf16[4096,512]{1,0:T(8,128)(2,1)} convert(f32[4096,512]{1,0:T(8,128)} %param.9) | non-fusion elementwise | flops 2097152 | bytes 12582912 | tf_op jit(solution)/shard_map/convert_element_type | solution.py:671
  6.9 1.0 copy-done
  7.9 2.6 convert_element_type.7
  10.5 481.1 %shard_map.93 = (bf16[16,4096,512]{2,1,0:T(8,128)(2,1)}, f32[4096,512]{1,0:T(8,128)}, f32[8,512,512]{2,1,0:T(8,128)}, bf16[2,4,512,512]{3,2,1,0:T(8,128)(2,1)}, bf16[2,512,512]{2,1,0:T(8,128)(2,1)}) custom-call(bf16[512,1024]{1,0:T(8,128)(2,1)} %bitcast.46, bf16[8,512,512]{2,1,0:T(8,128)(2,1)} %bitcast.43, bf16[8,512,512]{2,1,0:T(8,128)(2,1)} %bitcast.44, ...), custom_call_target="tpu_custom_call" | custom-call | tf_op jit(solution)/shard_map/pallas_call | solution.py:618
  491.5 0.0 slice-start.2
  491.6 0.0 slice-start.3
  491.6 7.9 %multiply_reduce_fusion.1 = (f32[]{:T(128)}, f32[]{:T(128)}) fusion(f32[4096,512]{1,0:T(8,128)} %get-tuple-element.13, f32[8,512,512]{2,1,0:T(8,128)} %get-tuple-element.14), kind=kLoop, calls=%fused_computation.6 | loop fusion | flops 12582910 | bytes 16777224 | tf_op jit(solution)/shard_map/reduce_sum | solution.py:675
  499.5 2.1 pad_maximum_fusion
  501.6 0.0 collective-permute-start
  501.6 0.1 slice_bitcast_fusion
  501.7 0.1 bitcast_dynamic-update-slice_fusion.7
  501.8 0.1 bitcast_dynamic-update-slice_fusion.6
  501.9 0.1 bitcast_dynamic-update-slice_fusion.5
  501.9 0.1 bitcast_dynamic-update-slice_fusion.4
  502.0 0.1 bitcast_dynamic-update-slice_fusion.3
  502.1 0.1 bitcast_dynamic-update-slice_fusion.2
  502.2 0.1 bitcast_dynamic-update-slice_fusion.1
  502.3 0.1 bitcast_dynamic-update-slice_fusion
  502.3 0.4 collective-permute-done
  502.7 1.4 fusion.5
  504.1 2.0 collective-permute-start.1
  506.1 6.2 %multiply_add_fusion.2 = f32[4096,512]{1,0:T(8,128)} fusion(f32[4096,512]{1,0:T(8,128)S(1)} %bitcast.40, bf16[512,4096]{1,0:T(8,128)(2,1)S(1)} %bitcast_dynamic-update-slice_fusion, bf16[512,512]{1,0:T(8,128)(2,1)S(1)} %get-tuple-element.16), kind=kOutput, calls=%fused_computation.4 | convolution fusion | flops 2153775104 | bytes 21495808 | tf_op jit(solution)/shard_map/dot_general | solution.py:19
  512.3 0.0 collective-permute-done.1
  512.4 0.0 slice-start.1
  512.4 0.4 collective-permute-start.2
  512.8 6.2 %multiply_add_fusion.1 = f32[4096,512]{1,0:T(8,128)} fusion(f32[4096,512]{1,0:T(8,128)S(1)} %bitcast.42, bf16[512,4096]{1,0:T(8,128)(2,1)S(1)} %bitcast_dynamic-update-slice_fusion, bf16[512,512]{1,0:T(8,128)(2,1)S(1)} %get-tuple-element.18), kind=kOutput, calls=%fused_computation.3 | convolution fusion | flops 2153775104 | bytes 21495808 | tf_op jit(solution)/shard_map/dot_general | solution.py:19
  519.0 0.0 collective-permute-done.2
  519.1 3.5 collective-permute-done.3
  522.6 4.4 collective-permute-done.4
  527.0 0.6 fusion
  529.0 11.1 %multiply_subtract_fusion = (f32[4096,512]{1,0:T(8,128)}, f32[4096,512]{1,0:T(8,128)}) fusion(f32[4096,512]{1,0:T(8,128)} %get-tuple-element.13, f32[8,512,512]{2,1,0:T(8,128)} %get-tuple-element.14, f32[]{:T(128)} %bitcast.17, f32[4096,512]{1,0:T(8,128)S(1)} %bitcast.38), kind=kLoop, calls=%fused_computation.1 | loop fusion | flops 12582912 | bytes 41943044 | tf_op jit(solution)/shard_map/sub | solution.py:684
  (22 shorter events, 0.0 us)
Async XLA Ops:
  0.6 7.3 %copy-start = (f32[4096,512]{1,0:T(8,128)S(1)}, f32[4096,512]{1,0:T(8,128)}, u32[]{:S(2)}) copy-start(f32[4096,512]{1,0:T(8,128)} %map_hbm.1) | copy-start | bytes 25165828
  491.5 14.6 %slice-start.2 = ((s8[8388608]{0:T(1024)(128)(4,1)}), s8[4194304]{0:T(1024)(128)(4,1)S(1)}, s32[]{:S(2)}) async-start(s8[8388608]{0:T(1024)(128)(4,1)} %bitcast.39), calls=%async_computation.2 | async-start | bytes 8388608
  491.5 10.1 %copy-start.2 = (bf16[2,512,512]{2,1,0:T(8,128)(2,1)S(1)}, bf16[2,512,512]{2,1,0:T(8,128)(2,1)}, u32[]{:S(2)}) copy-start(bf16[2,512,512]{2,1,0:T(8,128)(2,1)} %get-tuple-element.15) | copy-start | bytes 3145732
  491.6 10.2 %copy-start.1 = (bf16[2,4,512,512]{3,2,1,0:T(8,128)(2,1)S(1)}, bf16[2,4,512,512]{3,2,1,0:T(8,128)(2,1)}, u32[]{:S(2)}) copy-start(bf16[2,4,512,512]{3,2,1,0:T(8,128)(2,1)} %get-tuple-element.12) | copy-start | bytes 12582916
  491.6 14.6 %slice-start.3 = ((s8[8388608]{0:T(1024)(128)(4,1)}), s8[4194304]{0:T(1024)(128)(4,1)S(1)}, s32[]{:S(2)}) async-start(s8[8388608]{0:T(1024)(128)(4,1)} %bitcast.39), calls=%async_computation.3 | async-start | bytes 8388608
  501.6 1.1 collective-permute-start
  504.1 8.7 %slice-start.4 = ((s8[8388608]{0:T(1024)(128)(4,1)}), s8[4194304]{0:T(1024)(128)(4,1)S(1)}, s32[]{:S(2)}) async-start(s8[8388608]{0:T(1024)(128)(4,1)} %bitcast.41), calls=%async_computation.4 | async-start | bytes 8388608
  504.1 8.7 %slice-start.5 = ((s8[8388608]{0:T(1024)(128)(4,1)}), s8[4194304]{0:T(1024)(128)(4,1)S(1)}, s32[]{:S(2)}) async-start(s8[8388608]{0:T(1024)(128)(4,1)} %bitcast.41), calls=%async_computation.5 | async-start | bytes 8388608
  504.1 8.2 %collective-permute-start.1 = (f32[2]{0:T(128)S(1)}, f32[2]{0:T(128)S(1)}, u32[]{:S(2)}, u32[]{:S(2)}) collective-permute-start(f32[2]{0:T(128)S(1)} %fusion.5), channel_id=1, source_target_pairs={{0,1},{1,0},{2,3},{3,2},{4,5},{5,4},{6,7},{7,6},{8,9},{9,8},{10,11... | collective-permute-start | bytes 32 | tf_op jit(solution)/shard_map/ppermute | solution.py:33
  512.4 16.6 %slice-start = ((s8[8388608]{0:T(1024)(128)(4,1)}), s8[4194304]{0:T(1024)(128)(4,1)S(1)}, s32[]{:S(2)}) async-start(s8[8388608]{0:T(1024)(128)(4,1)} %bitcast.37), calls=%async_computation | async-start | bytes 8388608
  512.4 16.6 %slice-start.1 = ((s8[8388608]{0:T(1024)(128)(4,1)}), s8[4194304]{0:T(1024)(128)(4,1)S(1)}, s32[]{:S(2)}) async-start(s8[8388608]{0:T(1024)(128)(4,1)} %bitcast.37), calls=%async_computation.1 | async-start | bytes 8388608
  512.4 6.7 %collective-permute-start.2 = (f32[2]{0:T(128)S(1)}, f32[2]{0:T(128)S(1)}, u32[]{:S(2)}, u32[]{:S(2)}) collective-permute-start(f32[2]{0:T(128)S(1)} %add.30), channel_id=1, source_target_pairs={{0,2},{2,0},{4,6},{6,4},{8,10},{10,8},{12,14},{14,12},{1,3},{3,1},... | collective-permute-start | bytes 32 | tf_op jit(solution)/shard_map/ppermute | solution.py:33
  519.0 3.5 collective-permute-start.3
  522.6 4.4 collective-permute-start.4
